TPU v7x, 128 devices: a whole 4x4x4 slice. The times are simulated.
128 devices in a mesh: seq: 16 (over x, z), mp: 8 (over y, core).
Axes of the slice: x: 4, y: 4, z: 4, core: 2. Of those that a mesh axis runs over, the one named last changes fastest.
Arguments:
- tokens: bfloat16 [12288, 2560], P('seq', 'mp'), may hold values from -6 to 24
- norm_gain: float32 [2560], replicated, may hold values from 0.1 to 1.9
- w_query: bfloat16 [2560, 2048], P(None, 'mp'), may hold values from -0.25 to 0.25
- w_key: bfloat16 [2560, 2048], P(None, 'mp'), may hold values from -0.25 to 0.25
- w_value: bfloat16 [2560, 2048], P(None, 'mp'), may hold values from -0.125 to 0.125
- w_out: bfloat16 [2048, 2560], P('mp'), may hold values from -0.125 to 0.125
- w_up: bfloat16 [6, 2560, 1024], P(None, None, 'mp'), may hold values from -0.125 to 0.125
- w_class: bfloat16 [1024, 14], P('mp'), may hold values from -1 to 1
- starts: int32 [12288], P('seq'), may hold values from 0 to 63487, as said below
- lengths: int32 [12288], P('seq'), may hold values from 1 to 6, as said below
- labels: int32 [63488, 14], P('seq'), may hold values 0 or 1
Outputs:
- features: bfloat16 [63488, 1024], P('seq', 'mp')
- loss: float32 [63488], P('seq')
Inputs may be any that keep to these rules, and one draw needn't show every extreme that they name: starts are the running sums of lengths before each token, starting at 0. The tokens of seq index s cover positions from 3968 * s - 5 * d to 3968 * (s + 1) - 5 * e, where d is the value for index s - 1 and e the one for s, each 0 to 128; e is 0 for the last index and reaches 128 on some index. `lengths`: each length is 1 or 6; they sum to 63488; one seq index holds 0 to 256 tokens of length 1.
All inputs are finite; a program needn't handle non-finite values. No bound on the sum of `labels` on one device may be relied on, other than what follows from the above.
Results may differ from a plain program's by a relative error of at most 0.019.
Values may be sent and summed in bfloat16 or wider, within the bound.
A program may use at most 128 MiB of HBM per device.

v0:
```python
import math

import jax
import jax.numpy as jnp
from jax import lax
from jax.sharding import PartitionSpec as P

HD = 128
KMER = 6


def shifted(array, axis, by):
    devices = lax.axis_size(axis)
    pairs = [(i, i + by) for i in range(devices) if 0 <= i + by < devices]
    return lax.ppermute(array, axis, pairs)


def layer_norm(values, norm_gain):
    wide = values.astype(jnp.float32)
    row_mean = jnp.mean(wide, axis=-1, keepdims=True)
    centred = wide - row_mean
    variance = jnp.mean(centred * centred, axis=-1, keepdims=True)
    return (centred * lax.rsqrt(variance + 1e-05) * norm_gain).astype(jnp.bfloat16)


def attend_block(carry, query_heads, key_block, value_block, scale):
    running_max, running_total, numerator = carry
    local_heads = query_heads.shape[1]
    key_heads = key_block.reshape(key_block.shape[0], local_heads, HD)
    value_heads = value_block.reshape(value_block.shape[0], local_heads, HD)
    scores = (
        jnp.einsum("thd,rhd->htr", query_heads, key_heads, preferred_element_type=jnp.float32)
        * scale
    )
    new_max = jnp.maximum(running_max, jnp.max(scores, axis=-1))
    factor = jnp.exp(running_max - new_max)
    expos = jnp.exp(scores - new_max[:, :, None])
    new_total = running_total * factor + jnp.sum(expos, axis=-1)
    added = jnp.einsum(
        "htr,rhd->htd", expos.astype(jnp.bfloat16), value_heads, preferred_element_type=jnp.float32
    )
    return (new_max, new_total, numerator * factor[:, :, None] + added)


def per_device(
    tokens, norm_gain, w_query, w_key, w_value, w_out, w_up, w_class, starts, lengths, labels
):
    stream_full = lax.all_gather(tokens, "mp", axis=1, tiled=True)
    normed = layer_norm(stream_full, norm_gain)
    queries = jnp.dot(normed, w_query, preferred_element_type=jnp.float32).astype(jnp.bfloat16)
    keys = jnp.dot(normed, w_key, preferred_element_type=jnp.float32).astype(jnp.bfloat16)
    values = jnp.dot(normed, w_value, preferred_element_type=jnp.float32).astype(jnp.bfloat16)
    tok_rows = queries.shape[0]
    local_heads = queries.shape[1] // HD
    query_heads = queries.reshape(tok_rows, local_heads, HD)
    scale = 1.0 / math.sqrt(HD)
    block_rows = 1024
    initial = (
        jnp.full((local_heads, tok_rows), -1e30, jnp.float32),
        jnp.zeros((local_heads, tok_rows), jnp.float32),
        jnp.zeros((local_heads, tok_rows, HD), jnp.float32),
    )
    key_piece = lax.all_gather(keys, "seq", axis=0, tiled=True)
    value_piece = lax.all_gather(values, "seq", axis=0, tiled=True)
    piece_rows = key_piece.shape[0]

    def one_block(block_index, inner):
        key_block = lax.dynamic_slice_in_dim(key_piece, block_index * block_rows, block_rows, 0)
        value_block = lax.dynamic_slice_in_dim(value_piece, block_index * block_rows, block_rows, 0)
        return attend_block(inner, query_heads, key_block, value_block, scale)

    running_max, running_total, numerator = lax.fori_loop(
        0, piece_rows // block_rows, one_block, initial
    )
    attended = (numerator / running_total[:, :, None]).astype(jnp.bfloat16)
    attended = attended.transpose(1, 0, 2).reshape(tok_rows, local_heads * HD)
    partial_value = jnp.dot(attended, w_out, preferred_element_type=jnp.float32)
    stream = (
        stream_full.astype(jnp.float32)
        + lax.psum(partial_value.astype(jnp.bfloat16), "mp").astype(jnp.float32)
    ).astype(jnp.bfloat16)
    expanded = jax.nn.gelu(
        jnp.einsum("td,jdc->tjc", stream, w_up, preferred_element_type=jnp.float32)
    ).astype(jnp.bfloat16)
    local_channels = expanded.shape[2]
    nuc_rows = labels.shape[0]
    lead_rows = 5 * (tok_rows // 6)
    device_first = lax.axis_index("seq") * nuc_rows
    offsets = jnp.arange(KMER, dtype=jnp.int32)
    positions = starts[:, None] - device_first + lead_rows + offsets[None, :]
    live = offsets[None, :] < lengths[:, None]
    target = jnp.where(live, positions, lead_rows + nuc_rows).reshape(-1)
    placed = (
        jnp.zeros((lead_rows + nuc_rows, local_channels), jnp.bfloat16)
        .at[target]
        .set(expanded.reshape(-1, local_channels), mode="drop")
    )
    leading = placed[:lead_rows]
    own_rows = placed[lead_rows:]
    arriving = shifted(leading, "seq", -1)
    features = jnp.concatenate(
        [own_rows[: nuc_rows - lead_rows], own_rows[nuc_rows - lead_rows :] + arriving], axis=0
    )
    partial_logits = lax.dot_general(
        w_class, features, (((0,), (1,)), ((), ())), preferred_element_type=jnp.float32
    )
    logits = lax.psum(partial_logits.astype(jnp.bfloat16), "mp").astype(jnp.float32)
    picked = jnp.sum(labels.T.astype(jnp.float32) * logits, axis=0)
    return (features, jnp.sum(jax.nn.softplus(logits), axis=0) - picked)


def solution(mesh):
    return jax.shard_map(
        per_device,
        mesh=mesh,
        in_specs=(
            P("seq", "mp"),
            P(),
            P(None, "mp"),
            P(None, "mp"),
            P(None, "mp"),
            P("mp", None),
            P(None, None, "mp"),
            P("mp", None),
            P("seq"),
            P("seq"),
            P("seq", None),
        ),
        out_specs=(P("seq", "mp"), P("seq")),
        check_vma=False,
    )
```

profile of v0, /device:TPU:1, one launch (start us, length us, event | category | flops | bytes accessed | tf_op | source)
XLA Modules:
  0.0 559.9 jit_solution(7128170439297942995)
XLA Ops:
  8.0 36.4 %all-gather.4.cloned.1.call-done = bf16[768,2560]{0,1:T(8,128)(2,1)} async-done(((bf16[768,320]{0,1:T(8,128)(2,1)}), bf16[768,2560]{0,1:T(8,128)(2,1)}) %all-gather.4.cloned.1.call-update) | async-done | bytes 3932176 | tf_op jit(solution)/shard_map/all_gather | solution.py:48
  44.4 2.9 convert_reduce_fusion
  48.8 1.6 fusion.17
  50.4 1.9 copy-done.2
  52.3 2.0 convolution_convert_fusion.4
  54.4 4.1 convolution_convert_fusion.2
  58.7 3.7 convolution_convert_fusion.3
  62.7 52.6 %all-gather.6.cloned.1.call-done = bf16[12288,256]{1,0:T(8,128)(2,1)} async-done(((bf16[768,256]{1,0:T(8,128)(2,1)}), bf16[12288,256]{1,0:T(8,128)(2,1)}) %all-gather.6.cloned.1.call-update) | async-done | bytes 6291472 | tf_op jit(solution)/shard_map/all_gather | solution.py:63
  115.4 63.2 %all-gather.8.cloned.1.call-done = bf16[12288,256]{1,0:T(8,128)(2,1)} async-done(((bf16[768,256]{1,0:T(8,128)(2,1)}), bf16[12288,256]{1,0:T(8,128)(2,1)}) %all-gather.8.cloned.1.call-update) | async-done | bytes 6291472 | tf_op jit(solution)/shard_map/all_gather | solution.py:64
  178.6 206.4 %while.18 = (s32[]{:T(128)}, f32[2,768]{1,0:T(2,128)S(1)}, f32[2,768]{1,0:T(2,128)}, f32[2,768,128]{2,1,0:T(8,128)}, bf16[12288,256]{1,0:T(8,128)(2,1)}, /*index...) while((s32[]{:T(128)}, f32[2,768]{1,0:T(2,128)S(1)}, ...), condition=%wide.region_5.0_spmd.clone, body=%wide.region_2.0_spmd.clone.sunk | while | flops 818486784 | bytes 32547124 | solution.py:72
  178.6 1.3 constant_dynamic-slice_fusion.3
  180.1 4.2 bitcast_reduce_fusion.2
  185.1 3.8 fusion.69
  189.7 4.5 fusion.71
  195.1 1.3 constant_dynamic-slice_fusion.3
  196.6 4.2 bitcast_reduce_fusion.2
  201.6 3.8 fusion.69
  207.0 4.5 fusion.71
  213.9 4.2 bitcast_reduce_fusion.2
  218.9 3.8 fusion.69
  224.3 4.5 fusion.71
  229.6 1.3 constant_dynamic-slice_fusion.3
  231.1 4.2 bitcast_reduce_fusion.2
  236.1 3.8 fusion.69
  241.5 4.5 fusion.71
  246.9 1.3 constant_dynamic-slice_fusion.3
  248.4 4.2 bitcast_reduce_fusion.2
  253.4 3.8 fusion.69
  258.8 4.5 fusion.71
  264.2 1.3 constant_dynamic-slice_fusion.3
  265.6 4.2 bitcast_reduce_fusion.2
  270.7 3.8 fusion.69
  276.0 4.5 fusion.71
  281.4 1.3 constant_dynamic-slice_fusion.3
  282.9 4.2 bitcast_reduce_fusion.2
  287.9 3.8 fusion.69
  293.3 4.5 fusion.71
  298.7 1.3 constant_dynamic-slice_fusion.3
  300.1 4.2 bitcast_reduce_fusion.2
  305.2 3.8 fusion.69
  310.5 4.5 fusion.71
  315.9 1.3 constant_dynamic-slice_fusion.3
  317.4 4.2 bitcast_reduce_fusion.2
  322.4 3.8 fusion.69
  327.8 4.5 fusion.71
  333.2 1.3 constant_dynamic-slice_fusion.3
  334.7 4.2 bitcast_reduce_fusion.2
  339.7 3.8 fusion.69
  345.0 4.5 fusion.71
  350.4 1.3 constant_dynamic-slice_fusion.3
  351.9 4.2 bitcast_reduce_fusion.2
  356.9 3.8 fusion.69
  362.3 4.5 fusion.71
  369.2 4.2 bitcast_reduce_fusion.2
  374.2 3.8 fusion.69
  379.5 4.5 fusion.71
  384.9 1.4 copy.22
  387.1 3.1 convolution_convert_fusion
  391.2 68.7 %all-reduce.3.cloned.1.call-done = bf16[768,2560]{0,1:T(8,128)(2,1)} async-done(((bf16[768,2560]{0,1:T(8,128)(2,1)}), bf16[768,2560]{0,1:T(8,128)(2,1)}) %all-reduce.3.cloned.1.call-update) | async-done | bytes 3932176 | tf_op jit(solution)/shard_map/psum | solution.py:80
  459.9 8.2 %fusion.30 = bf16[768,6,128]{2,0,1:T(8,128)(2,1)S(1)} fusion(bf16[6,2560,128]{2,1,0:T(8,128)(2,1)} %param.19, bf16[768,2560]{0,1:T(8,128)(2,1)} %all-reduce.3.cloned.1.call-done, bf16[768,2560]{0,1:T(8,128)(2,1)} %all-gather.4.cloned.1.call-done), kind=kOutput, calls=%fused_computation.41 | convolution fusion | flops 3033071616 | bytes 12976128 | tf_op jit(solution)/shard_map/td,jdc->tjc/dot_general | solution.py:83
  470.1 12.8 %scatter_custom_fusion = bf16[4608,128]{1,0:T(8,128)(2,1)S(1)} fusion(s32[4608]{0:T(1024)S(1)} %fusion.41, bf16[4608,128]{1,0:T(8,128)(2,1)} %reshape.109, bf16[]{:T(256)} %constant.71.clone.1), kind=kCustom, calls=%fused_computation.48 | custom fusion | bytes 1180160 | tf_op jit(solution)/shard_map/scatter | solution.py:96
  482.9 1.3 collective-permute-start
  484.3 4.7 collective-permute-done
  490.2 61.4 %all-reduce.5.cloned.1.call-done = bf16[14,3968]{1,0:T(8,128)(2,1)} async-done(((bf16[14,3968]{1,0:T(8,128)(2,1)}), bf16[14,3968]{1,0:T(8,128)(2,1)}) %all-reduce.5.cloned.1.call-update) | async-done | bytes 111120 | tf_op jit(solution)/shard_map/psum | solution.py:107
  (234 shorter events, 51.8 us)
Async XLA Ops:
  7.2 379.9 %copy-start = (bf16[256,2560]{1,0:T(8,128)(2,1)S(1)}, bf16[256,2560]{1,0:T(8,128)(2,1)}, u32[]{:S(2)}) copy-start(bf16[256,2560]{1,0:T(8,128)(2,1)} %param.18) | copy-start | bytes 3932164
  7.2 37.2 %all-gather.4.cloned.1.call-start = ((), (), s32[]{:S(2)}) async-start(), calls=%async_computation | async-start | bytes 4423680 | tf_op jit(solution)/shard_map/all_gather | solution.py:48
  7.9 40.9 %copy-start.12 = (f32[2560]{0:T(1024)S(1)}, f32[2560]{0:T(1024)}, u32[]{:S(2)}) copy-start(f32[2560]{0:T(1024)} %param.14) | copy-start | bytes 30724
  7.9 107.4 %all-gather.6.cloned.1.call-start = ((), (), s32[]{:S(2)}) async-start(), calls=%async_computation.1 | async-start | bytes 6684672 | tf_op jit(solution)/shard_map/all_gather | solution.py:63
  44.4 3.3 copy-start.1
  48.8 3.5 copy-start.6
  50.4 1.9 copy-start.2
  52.3 2.1 copy-start.7
  54.3 124.3 %all-gather.8.cloned.1.call-start = ((), (), s32[]{:S(2)}) async-start(), calls=%async_computation.2 | async-start | bytes 6684672 | tf_op jit(solution)/shard_map/all_gather | solution.py:64
  58.5 401.4 %all-reduce.3.cloned.1.call-start = ((), (), s32[]{:S(2)}) async-start(), calls=%async_computation.3 | async-start | bytes 7864320 | tf_op jit(solution)/shard_map/psum | solution.py:80
  178.6 5.7 %copy-start.8 = (f32[2,768]{1,0:T(2,128)}, f32[2,768]{1,0:T(2,128)S(1)}, u32[]{:S(2)}) copy-start(f32[2,768]{1,0:T(2,128)S(1)} %get-tuple-element.256) | copy-start | bytes 18436 | tf_op jit(solution)/shard_map/while
  184.3 4.6 copy-start.10
  184.3 5.5 copy-start.3
  194.3 0.9 copy-start.4
  195.1 5.7 %copy-start.8 = (f32[2,768]{1,0:T(2,128)}, f32[2,768]{1,0:T(2,128)S(1)}, u32[]{:S(2)}) copy-start(f32[2,768]{1,0:T(2,128)S(1)} %get-tuple-element.256) | copy-start | bytes 18436 | tf_op jit(solution)/shard_map/while
  200.9 4.6 copy-start.10
  200.9 6.1 %copy-start.3 = (f32[2,768,128]{2,1,0:T(8,128)S(1)}, f32[2,768,128]{2,1,0:T(8,128)}, u32[]{:S(2)}) copy-start(f32[2,768,128]{2,1,0:T(8,128)} %get-tuple-element.258) | copy-start | bytes 2359300 | tf_op jit(solution)/shard_map/while
  211.5 0.9 copy-start.4
  212.4 5.7 %copy-start.8 = (f32[2,768]{1,0:T(2,128)}, f32[2,768]{1,0:T(2,128)S(1)}, u32[]{:S(2)}) copy-start(f32[2,768]{1,0:T(2,128)S(1)} %get-tuple-element.256) | copy-start | bytes 18436 | tf_op jit(solution)/shard_map/while
  218.1 4.6 copy-start.10
  218.1 6.1 %copy-start.3 = (f32[2,768,128]{2,1,0:T(8,128)S(1)}, f32[2,768,128]{2,1,0:T(8,128)}, u32[]{:S(2)}) copy-start(f32[2,768,128]{2,1,0:T(8,128)} %get-tuple-element.258) | copy-start | bytes 2359300 | tf_op jit(solution)/shard_map/while
  228.8 0.9 copy-start.4
  229.6 5.7 %copy-start.8 = (f32[2,768]{1,0:T(2,128)}, f32[2,768]{1,0:T(2,128)S(1)}, u32[]{:S(2)}) copy-start(f32[2,768]{1,0:T(2,128)S(1)} %get-tuple-element.256) | copy-start | bytes 18436 | tf_op jit(solution)/shard_map/while
  235.4 4.6 copy-start.10
  235.4 6.1 %copy-start.3 = (f32[2,768,128]{2,1,0:T(8,128)S(1)}, f32[2,768,128]{2,1,0:T(8,128)}, u32[]{:S(2)}) copy-start(f32[2,768,128]{2,1,0:T(8,128)} %get-tuple-element.258) | copy-start | bytes 2359300 | tf_op jit(solution)/shard_map/while
  246.0 0.9 copy-start.4
  246.9 5.7 %copy-start.8 = (f32[2,768]{1,0:T(2,128)}, f32[2,768]{1,0:T(2,128)S(1)}, u32[]{:S(2)}) copy-start(f32[2,768]{1,0:T(2,128)S(1)} %get-tuple-element.256) | copy-start | bytes 18436 | tf_op jit(solution)/shard_map/while
  252.6 4.6 copy-start.10
  252.6 6.1 %copy-start.3 = (f32[2,768,128]{2,1,0:T(8,128)S(1)}, f32[2,768,128]{2,1,0:T(8,128)}, u32[]{:S(2)}) copy-start(f32[2,768,128]{2,1,0:T(8,128)} %get-tuple-element.258) | copy-start | bytes 2359300 | tf_op jit(solution)/shard_map/while
  263.3 0.9 copy-start.4
  264.2 5.7 %copy-start.8 = (f32[2,768]{1,0:T(2,128)}, f32[2,768]{1,0:T(2,128)S(1)}, u32[]{:S(2)}) copy-start(f32[2,768]{1,0:T(2,128)S(1)} %get-tuple-element.256) | copy-start | bytes 18436 | tf_op jit(solution)/shard_map/while
  269.9 4.6 copy-start.10
  269.9 6.1 %copy-start.3 = (f32[2,768,128]{2,1,0:T(8,128)S(1)}, f32[2,768,128]{2,1,0:T(8,128)}, u32[]{:S(2)}) copy-start(f32[2,768,128]{2,1,0:T(8,128)} %get-tuple-element.258) | copy-start | bytes 2359300 | tf_op jit(solution)/shard_map/while
  280.5 0.9 copy-start.4
  281.4 5.7 %copy-start.8 = (f32[2,768]{1,0:T(2,128)}, f32[2,768]{1,0:T(2,128)S(1)}, u32[]{:S(2)}) copy-start(f32[2,768]{1,0:T(2,128)S(1)} %get-tuple-element.256) | copy-start | bytes 18436 | tf_op jit(solution)/shard_map/while
  287.1 4.6 copy-start.10
  287.1 6.1 %copy-start.3 = (f32[2,768,128]{2,1,0:T(8,128)S(1)}, f32[2,768,128]{2,1,0:T(8,128)}, u32[]{:S(2)}) copy-start(f32[2,768,128]{2,1,0:T(8,128)} %get-tuple-element.258) | copy-start | bytes 2359300 | tf_op jit(solution)/shard_map/while
  297.8 0.9 copy-start.4
  298.7 5.7 %copy-start.8 = (f32[2,768]{1,0:T(2,128)}, f32[2,768]{1,0:T(2,128)S(1)}, u32[]{:S(2)}) copy-start(f32[2,768]{1,0:T(2,128)S(1)} %get-tuple-element.256) | copy-start | bytes 18436 | tf_op jit(solution)/shard_map/while
  304.4 4.6 copy-start.10
  304.4 6.1 %copy-start.3 = (f32[2,768,128]{2,1,0:T(8,128)S(1)}, f32[2,768,128]{2,1,0:T(8,128)}, u32[]{:S(2)}) copy-start(f32[2,768,128]{2,1,0:T(8,128)} %get-tuple-element.258) | copy-start | bytes 2359300 | tf_op jit(solution)/shard_map/while
  315.0 0.9 copy-start.4
  315.9 5.7 %copy-start.8 = (f32[2,768]{1,0:T(2,128)}, f32[2,768]{1,0:T(2,128)S(1)}, u32[]{:S(2)}) copy-start(f32[2,768]{1,0:T(2,128)S(1)} %get-tuple-element.256) | copy-start | bytes 18436 | tf_op jit(solution)/shard_map/while
  321.6 4.6 copy-start.10
  321.6 6.1 %copy-start.3 = (f32[2,768,128]{2,1,0:T(8,128)S(1)}, f32[2,768,128]{2,1,0:T(8,128)}, u32[]{:S(2)}) copy-start(f32[2,768,128]{2,1,0:T(8,128)} %get-tuple-element.258) | copy-start | bytes 2359300 | tf_op jit(solution)/shard_map/while
  332.3 0.9 copy-start.4
  333.2 5.7 %copy-start.8 = (f32[2,768]{1,0:T(2,128)}, f32[2,768]{1,0:T(2,128)S(1)}, u32[]{:S(2)}) copy-start(f32[2,768]{1,0:T(2,128)S(1)} %get-tuple-element.256) | copy-start | bytes 18436 | tf_op jit(solution)/shard_map/while
  338.9 4.6 copy-start.10
  338.9 6.1 %copy-start.3 = (f32[2,768,128]{2,1,0:T(8,128)S(1)}, f32[2,768,128]{2,1,0:T(8,128)}, u32[]{:S(2)}) copy-start(f32[2,768,128]{2,1,0:T(8,128)} %get-tuple-element.258) | copy-start | bytes 2359300 | tf_op jit(solution)/shard_map/while
  349.5 0.9 copy-start.4
  350.4 5.7 %copy-start.8 = (f32[2,768]{1,0:T(2,128)}, f32[2,768]{1,0:T(2,128)S(1)}, u32[]{:S(2)}) copy-start(f32[2,768]{1,0:T(2,128)S(1)} %get-tuple-element.256) | copy-start | bytes 18436 | tf_op jit(solution)/shard_map/while
  356.1 4.6 copy-start.10
  356.1 6.1 %copy-start.3 = (f32[2,768,128]{2,1,0:T(8,128)S(1)}, f32[2,768,128]{2,1,0:T(8,128)}, u32[]{:S(2)}) copy-start(f32[2,768,128]{2,1,0:T(8,128)} %get-tuple-element.258) | copy-start | bytes 2359300 | tf_op jit(solution)/shard_map/while
  366.8 0.9 copy-start.4
  367.7 5.7 %copy-start.8 = (f32[2,768]{1,0:T(2,128)}, f32[2,768]{1,0:T(2,128)S(1)}, u32[]{:S(2)}) copy-start(f32[2,768]{1,0:T(2,128)S(1)} %get-tuple-element.256) | copy-start | bytes 18436 | tf_op jit(solution)/shard_map/while
  373.4 4.6 copy-start.10
  373.4 6.1 %copy-start.3 = (f32[2,768,128]{2,1,0:T(8,128)S(1)}, f32[2,768,128]{2,1,0:T(8,128)}, u32[]{:S(2)}) copy-start(f32[2,768,128]{2,1,0:T(8,128)} %get-tuple-element.258) | copy-start | bytes 2359300 | tf_op jit(solution)/shard_map/while
  387.1 3.4 copy-start.15
  387.1 3.4 copy-start.13
  390.3 161.3 %all-reduce.5.cloned.1.call-start = ((), (), s32[]{:S(2)}) async-start(), calls=%async_computation.4 | async-start | bytes 253952 | tf_op jit(solution)/shard_map/psum | solution.py:107
  468.9 20.2 %copy-start.14 = (bf16[128,14]{0,1:T(8,128)(2,1)S(1)}, bf16[128,14]{0,1:T(8,128)(2,1)}, u32[]{:S(2)}) copy-start(bf16[128,14]{0,1:T(8,128)(2,1)} %param.20) | copy-start | bytes 10756
  470.1 81.4 %copy-start.9 = (s32[3968,14]{0,1:T(8,128)S(1)}, s32[3968,14]{0,1:T(8,128)}, u32[]{:S(2)}) copy-start(s32[3968,14]{0,1:T(8,128)} %param.23) | copy-start | bytes 666628
  482.9 6.1 %collective-permute-start = (bf16[640,128]{1,0:T(8,128)(2,1)S(1)}, bf16[640,128]{1,0:T(8,128)(2,1)S(1)}, u32[]{:S(2)}, u32[]{:S(2)}) collective-permute-start(bf16[640,128]{1,0:T(8,128)(2,1)S(1)} %slice.17), channel_id=1, source_target_pairs={{8,0},{16,8},{24,16},{32,24},{40,32},{48,40},{56,48},{64,56},{72,6... | collective-permute-start | bytes 491528 | tf_op jit(solution)/shard_map/ppermute | solution.py:15
  489.1 64.2 %copy-start.5 = (bf16[3968,128]{1,0:T(8,128)(2,1)}, bf16[3968,128]{1,0:T(8,128)(2,1)S(1)}, u32[]{:S(2)}) copy-start(bf16[3968,128]{1,0:T(8,128)(2,1)S(1)} %pad_maximum_fusion) | copy-start | bytes 3047428
  (13 other events, 8.0 us)
Sparse Core Ops, SparseCore 0:
  9.7 34.6 all-gather.3
  54.4 60.8 all-gather.5
  117.5 60.9 all-gather.7
  390.4 69.4 all-reduce.2
  490.3 61.2 all-reduce.4
where the time goes:
time: 564 us; the launch traced here: 560 us
  waiting for transfers between devices  288 us (51%)
  matrix products  127 us (23%)
  other arithmetic  71.5 us (13%)
  local copies, waits for them, and re-layouts  56.8 us (10%)
  between operations  14 us (2%)
    psum x1, waiting for transfers between devices, per_device(): lax.psum(partial_value.astype(jnp.bfloat16), 'mp').astype(jnp.float32)  68.7 us
    all_gather x1, waiting for transfers between devices, per_device(): value_piece = lax.all_gather(values, 'seq', axis=0, tiled=True)  63.2 us
    psum x1, waiting for transfers between devices, per_device(): lax.psum(partial_logits.astype(jnp.bfloat16), 'mp').astype(jnp.float32)  61.4 us
    dot_general x12, matrix products, attend_block(): jnp.einsum('htr,rhd->htd', expos.astype(jnp.bfloat16), value_heads, prefe...  54 us
    all_gather x1, waiting for transfers between devices, per_device(): key_piece = lax.all_gather(keys, 'seq', axis=0, tiled=True)  52.6 us
    dot_general x12, matrix products, attend_block(): jnp.einsum('thd,rhd->htr', query_heads, key_heads, preferred_element_type...  50.8 us
    reduce_sum x12, other arithmetic, attend_block(): new_total = running_total * factor + jnp.sum(expos, axis=-1)  45.8 us
    all_gather x1, waiting for transfers between devices, per_device(): stream_full = lax.all_gather(tokens, 'mp', axis=1, tiled=True)  36.4 us
  transfers between devices with their start and end apart: 6, of which 6 were waited for; matrix products, arithmetic and copies ran while one was open for 2% of the time, Pallas kernels for 0%

commit v1 on v0

v1 whole, which is shorter than its diff:
```python
import functools
import math

import jax
import jax.numpy as jnp
from jax import lax
from jax.experimental import pallas as pl
from jax.experimental.pallas import tpu as pltpu
from jax.sharding import PartitionSpec as P

HD = 128
KMER = 6
TOK = 768
D = 2560
NUC = 3968
LEAD = 640
PIECE = 512
PARTS = 8
CLASSES = 14
MESH = pl.DeviceIdType.MESH
ANY = pl.BlockSpec(memory_space=pl.ANY)
VMEM = pl.BlockSpec(memory_space=pltpu.VMEM)
SMEM = pl.BlockSpec(memory_space=pltpu.SMEM)
BF16 = jnp.bfloat16
F32 = jnp.float32
NT = (((1,), (1,)), ((), ()))


def coords():
    seq = lax.axis_index("seq")
    mp = lax.axis_index("mp")
    return seq // 4, mp // 2, seq % 4, mp % 2


def device(x, y, z, core):
    return {"seq": x * 4 + z, "mp": y * 2 + core}


def greet(partners):
    barrier = pltpu.get_barrier_semaphore()
    for partner in partners:
        pl.semaphore_signal(barrier, inc=1, device_id=partner, device_id_type=MESH)
    pl.semaphore_wait(barrier, len(partners))


def remote(src, dst, send_sem, recv_sem, target):
    return pltpu.make_async_remote_copy(
        src_ref=src, dst_ref=dst, send_sem=send_sem, recv_sem=recv_sem, device_id=target, device_id_type=MESH
    )


class Gather:
    def __init__(self, src, buf, rows, chunks, y_send, y_recv, f_send, f_recv, c_send, c_recv):
        self.src, self.buf, self.step = src, buf, rows // chunks
        self.chunks = chunks
        self.sems = (y_send, y_recv, f_send, f_recv, c_send, c_recv)
        x, y, z, core = coords()
        up, down, far = (y + 1) % 4, (y + 3) % 4, (y + 2) % 4
        self.up, self.down = device(x, up, z, core), device(x, down, z, core)
        self.sibling = device(x, y, z, 1 - core)
        self.own = y * 2 + core
        self.slots = [y * 2 + core, down * 2 + core, up * 2 + core, far * 2 + core]
        self.twins = [y * 2 + 1 - core, down * 2 + 1 - core, up * 2 + 1 - core, far * 2 + 1 - core]

    def partners(self):
        return [self.up, self.down, self.sibling]

    def rows(self, r, part=None):
        if part is None:
            return pl.ds(r * self.step, self.step)
        half = self.step // 2
        return pl.ds(r * self.step + part * half, half)

    def around(self, way, r):
        y_send, y_recv = self.sems[:2]
        rows = self.rows(r)
        return remote(
            self.src.at[rows], self.buf.at[self.own, rows], y_send.at[way, r], y_recv.at[way, r],
            self.up if way == 0 else self.down,
        )

    def arrived(self, way, r):
        y_send, y_recv = self.sems[:2]
        rows = self.rows(r)
        slot = self.buf.at[self.slots[1 + way], rows]
        return remote(slot, slot, y_send.at[way, r], y_recv.at[way, r], self.up if way == 0 else self.down)

    def onward(self, way, r):
        f_send, f_recv = self.sems[2:4]
        slot = self.buf.at[self.slots[1 + way], self.rows(r, way)]
        return remote(slot, slot, f_send.at[way, r], f_recv.at[way, r], self.up if way == 0 else self.down)

    def far_arrived(self, way, r):
        f_send, f_recv = self.sems[2:4]
        slot = self.buf.at[self.slots[3], self.rows(r, way)]
        return remote(slot, slot, f_send.at[way, r], f_recv.at[way, r], self.up if way == 0 else self.down)

    def across(self, which, r, arriving=False):
        c_send, c_recv = self.sems[4:]
        part = which - 3 if which >= 3 else None
        rows = self.rows(r, part)
        slots = self.twins if arriving else self.slots
        slot = self.buf.at[slots[min(which, 3)], rows]
        src = self.src.at[rows] if which == 0 and not arriving else slot
        return remote(src, slot, c_send.at[which, r], c_recv.at[which, r], self.sibling)

    def start(self):
        for r in range(self.chunks):
            self.around(0, r).start()
            self.around(1, r).start()
            self.across(0, r).start()

    def forward(self, r):
        for way in range(2):
            self.arrived(way, r).wait_recv()
            self.onward(way, r).start()
            self.across(1 + way, r).start()

    def forward_far(self, r):
        for way in range(2):
            self.far_arrived(way, r).wait_recv()
            self.across(3 + way, r).start()

    def complete(self, r):
        for which in range(5):
            self.across(which, r, arriving=True).wait_recv()

    def sent(self):
        for r in range(self.chunks):
            for way in range(2):
                self.around(way, r).wait_send()
                self.onward(way, r).wait_send()
            for which in range(5):
                self.across(which, r).wait_send()


def gather_sems(chunks):
    dma = pltpu.SemaphoreType.DMA
    return [dma((2, chunks)), dma((2, chunks)), dma((2, chunks)), dma((2, chunks)), dma((5, chunks)), dma((5, chunks))]


def qkv_kernel(
    tokens, gain, w_query, w_key, w_value, tok_full, q_out, k_out, v_out,
    blocks, weights, rows_v, local, *sems,
):
    chunks = 3
    step = TOK // chunks
    ring = Gather(tokens, blocks, TOK, chunks, *sems)
    own = pltpu.make_async_copy(tokens, blocks.at[ring.own], local.at[0])
    own.start()
    loads = [
        pltpu.make_async_copy(w, weights.at[:, pl.ds(i * 256, 256)], local.at[1 + i])
        for i, w in enumerate((w_query, w_key, w_value))
    ]
    for load in loads:
        load.start()
    greet(ring.partners())
    ring.start()
    own.wait()
    scale = math.log2(math.e) / math.sqrt(HD)
    stores = []
    for r in range(chunks + 1):
        if r < chunks:
            ring.forward(r)
        if r == 0:
            for load in loads:
                load.wait()
            continue
        done = r - 1
        ring.forward_far(done)
        ring.complete(done)
        rows = pl.ds(done * step, step)
        for j in range(PARTS):
            rows_v[rows, pl.ds(j * 320, 320)] = blocks[j, rows, :]
        store = pltpu.make_async_copy(rows_v.at[rows], tok_full.at[rows], local.at[4 + done])
        store.start()
        stores.append(store)
        wide = rows_v[rows, :].astype(F32)
        centred = wide - jnp.mean(wide, axis=-1, keepdims=True)
        variance = jnp.mean(centred * centred, axis=-1, keepdims=True)
        normed = (centred * lax.rsqrt(variance + 1e-05) * gain[...]).astype(BF16)
        qkv = jnp.dot(normed, weights[...], preferred_element_type=F32)
        q_out[:, rows] = (qkv[:, :256] * scale).T.astype(BF16)
        for h in range(2):
            k_out[h, rows, :] = qkv[:, 256 + h * HD : 256 + (h + 1) * HD].astype(BF16)
        v_out[:, rows] = qkv[:, 512:].T.astype(BF16)
    ring.sent()
    for store in stores:
        store.wait()


def project(tokens, gain, w_query, w_key, w_value):
    return pl.pallas_call(
        qkv_kernel,
        out_shape=(
            jax.ShapeDtypeStruct((TOK, D), BF16),
            jax.ShapeDtypeStruct((256, TOK), BF16),
            jax.ShapeDtypeStruct((2, TOK, HD), BF16),
            jax.ShapeDtypeStruct((256, TOK), BF16),
        ),
        in_specs=[ANY, VMEM, ANY, ANY, ANY],
        out_specs=(ANY, VMEM, VMEM, VMEM),
        scratch_shapes=[
            pltpu.VMEM((PARTS, TOK, 320), BF16),
            pltpu.VMEM((D, 768), BF16),
            pltpu.VMEM((TOK, D), BF16),
            pltpu.SemaphoreType.DMA((7,)),
            *gather_sems(3),
        ],
        compiler_params=pltpu.CompilerParams(
            collective_id=0, has_side_effects=True, vmem_limit_bytes=56 << 20
        ),
    )(tokens, gain, w_query, w_key, w_value)


def pick(index, options):
    value = options[-1]
    for i in range(len(options) - 2, -1, -1):
        value = jnp.where(index == i, options[i], value)
    return value


UNITS = [
    (0, 0), (1, 0), (2, 0), (0, 1), (1, 1), (2, 1), (0, 2), (1, 2), (2, 2),
    (3, 0), (3, 1), (3, 2), (3, 3), (1, 3), (2, 3), (0, 3),
]


def attend_kernel(
    q_in, k_in, v_in, w_out, att, w_full,
    qb, kb, vb, acc, top, o_send, l_send, o_recv, l_recv,
    local, q_ss, q_rs, k_ss, k_rs, v_ss, v_rs, o_ss, o_rs, l_ss, l_rs, *sems,
):
    x, y, z, core = coords()
    ring = Gather(w_out, w_full, 256, 2, *sems)

    def along(axis, by):
        if axis == 0:
            return device((x + by + 4) % 4, y, z, core)
        return device(x, y, (z + by + 4) % 4, core)

    offsets = {1: 1, 2: -1, 3: 2}

    def move(kind, h, slot):
        axis = 1 - h if kind == "q" else h
        target = along(axis, -offsets[slot])
        if kind == "q":
            src, dst, ss, rs = q_in.at[pl.ds(h * HD, HD)], qb.at[h, slot], q_ss, q_rs
        elif kind == "k":
            src, dst, ss, rs = k_in.at[h], kb.at[h, slot], k_ss, k_rs
        else:
            src, dst, ss, rs = v_in.at[pl.ds(h * HD, HD)], vb.at[h, slot], v_ss, v_rs
        return remote(src, dst, ss.at[h, slot], rs.at[h, slot], target)

    own = []
    for h in range(2):
        own.append(pltpu.make_async_copy(q_in.at[pl.ds(h * HD, HD)], qb.at[h, 0], local.at[0, h]))
        own.append(pltpu.make_async_copy(k_in.at[h], kb.at[h, 0], local.at[1, h]))
        own.append(pltpu.make_async_copy(v_in.at[pl.ds(h * HD, HD)], vb.at[h, 0], local.at[2, h]))
    own_w = pltpu.make_async_copy(w_out, w_full.at[ring.own], local.at[3, 0])
    for copy in own:
        copy.start()
    own_w.start()
    greet([along(a, by) for a in range(2) for by in (1, -1, 2)] + ring.partners())
    for kinds, slots in (("q", (1, 2)), ("kv", (1, 2)), ("q", (3,)), ("kv", (3,))):
        for slot in slots:
            for kind in kinds:
                for h in range(2):
                    move(kind, h, slot).start()
    ring.start()
    top[...] = jnp.full(top.shape, -1e30, F32)
    acc[...] = jnp.zeros(acc.shape, F32)
    for copy in own:
        copy.wait()

    ones = jnp.ones((16, TOK), BF16)

    def partial(h, a):
        total = acc[h, a, HD : HD + 8, :]
        return acc[h, a, :HD, :] / total[:1], top[h, a] + jnp.log2(total)

    def give(h, slot):
        by = pick(slot - 1, [1, -1, 2])
        target = along(1 - h, by)
        return [
            remote(o_send.at[h, slot - 1], o_recv.at[h, slot - 1], o_ss.at[h, slot - 1], o_rs.at[h, slot - 1], target),
            remote(l_send.at[h, slot - 1], l_recv.at[h, slot - 1], l_ss.at[h, slot - 1], l_rs.at[h, slot - 1], target),
        ]

    def unit(i, carry):
        def arrivals(kinds, slot):
            for kind in kinds:
                for h in range(2):
                    move(kind, h, slot).wait_recv()

        for index, kinds, slot in ((1, "q", 1), (2, "q", 2), (3, "kv", 1), (6, "kv", 2), (9, "q", 3), (12, "kv", 3)):
            pl.when(i == index)(functools.partial(arrivals, kinds, slot))
        pl.when(i == 7)(functools.partial(ring.forward, 0))
        pl.when(i == 13)(functools.partial(ring.forward, 1))
        a = pick(i, [u[0] for u in UNITS])
        b = pick(i, [u[1] for u in UNITS])
        scores = [
            jnp.dot(kb[h, b], qb[h, a], preferred_element_type=F32) for h in range(2)
        ]
        for h in range(2):
            s = scores[h]
            before = top[h, a]
            now = jnp.maximum(before, jnp.max(s, axis=0, keepdims=True))
            weights = jnp.exp2(s - now[:1]).astype(BF16)
            factor = jnp.exp2(before - now)
            lhs = jnp.concatenate([vb[h, b], ones], axis=0)
            added = jnp.dot(lhs, weights, preferred_element_type=F32)
            acc[h, a] = acc[h, a] * factor[:1] + added
            top[h, a] = now

        @pl.when(jnp.logical_and(i >= 12, i < 15))
        def _():
            for h in range(2):
                value, level = partial(h, a)
                o_send[h, a - 1] = value.astype(BF16)
                l_send[h, a - 1] = level
                for copy in give(h, a):
                    copy.start()

        return carry

    lax.fori_loop(0, len(UNITS), unit, 0)
    for r in range(2):
        ring.forward_far(r)
    for h in range(2):
        value, level = partial(h, 0)
        for slot in range(1, 4):
            for copy in give(h, slot):
                copy.wait_recv()
        levels = [level] + [l_recv[h, i] for i in range(3)]
        highest = functools.reduce(jnp.maximum, levels)
        shares = [jnp.exp2(one - highest) for one in levels]
        total = functools.reduce(jnp.add, shares)
        shares = [share / total for share in shares]
        value = value * shares[0][:1]
        for i in range(3):
            value = value + o_recv[h, i].astype(F32) * shares[1 + i][:1]
        att[:, pl.ds(h * HD, HD)] = value.T.astype(BF16)
    own_w.wait()
    for r in range(2):
        ring.complete(r)
    ring.sent()
    for h in range(2):
        for slot in range(1, 4):
            for kind in "qkv":
                move(kind, h, slot).wait_send()
            for copy in give(h, slot):
                copy.wait_send()


def attend(q, k, v, w_out):
    dma = pltpu.SemaphoreType.DMA
    return pl.pallas_call(
        attend_kernel,
        out_shape=(
            jax.ShapeDtypeStruct((TOK, 256), BF16),
            jax.ShapeDtypeStruct((PARTS, 256, D), BF16),
        ),
        in_specs=[ANY] * 4,
        out_specs=(VMEM, ANY),
        scratch_shapes=[
            pltpu.VMEM((2, 4, HD, TOK), BF16),
            pltpu.VMEM((2, 4, TOK, HD), BF16),
            pltpu.VMEM((2, 4, HD, TOK), BF16),
            pltpu.VMEM((2, 4, HD + 16, TOK), F32),
            pltpu.VMEM((2, 4, 8, TOK), F32),
            pltpu.VMEM((2, 3, HD, TOK), BF16),
            pltpu.VMEM((2, 3, 8, TOK), F32),
            pltpu.VMEM((2, 3, HD, TOK), BF16),
            pltpu.VMEM((2, 3, 8, TOK), F32),
            dma((4, 2)),
            *[dma((2, 4)) for _ in range(6)],
            *[dma((2, 3)) for _ in range(4)],
            *gather_sems(2),
        ],
        compiler_params=pltpu.CompilerParams(
            collective_id=1, has_side_effects=True, vmem_limit_bytes=56 << 20
        ),
    )(q, k, v, w_out)


def gelu(x):
    return 0.5 * x * (1.0 + jnp.tanh(math.sqrt(2.0 / math.pi) * (x + 0.044715 * x * x * x)))


def expand_kernel(att, tok, w_full, w_up, out, blocks, wo_v, wu_v, tok_v, local, *sems):
    chunks = 3
    step = TOK // chunks
    ring = Gather(att, blocks, TOK, chunks, *sems)
    loads = [pltpu.make_async_copy(att, blocks.at[ring.own], local.at[0])]
    loads += [pltpu.make_async_copy(tok, tok_v, local.at[1])]
    loads += [
        pltpu.make_async_copy(w_up.at[j], wu_v.at[:, pl.ds(j * HD, HD)], local.at[2 + j]) for j in range(KMER)
    ]
    loads += [
        pltpu.make_async_copy(w_full.at[j], wo_v.at[pl.ds(j * 256, 256)], local.at[8 + j]) for j in range(PARTS)
    ]
    for load in loads:
        load.start()
    greet(ring.partners())
    ring.start()
    for r in range(chunks + 1):
        if r < chunks:
            ring.forward(r)
        if r == 0:
            for load in loads:
                load.wait()
            continue
        done = r - 1
        ring.forward_far(done)
        ring.complete(done)
        rows = pl.ds(done * step, step)
        joined = jnp.concatenate([blocks[j, rows, :] for j in range(PARTS)], axis=1)
        projected = jnp.dot(joined, wo_v[...], preferred_element_type=F32)
        stream = (tok_v[rows, :].astype(F32) + projected).astype(BF16)
        raised = jnp.dot(stream, wu_v[...], preferred_element_type=F32)
        out[rows, :] = gelu(raised).astype(BF16)
    ring.sent()


def expand(att, tok, w_full, w_up):
    return pl.pallas_call(
        expand_kernel,
        out_shape=jax.ShapeDtypeStruct((TOK, KMER * HD), BF16),
        in_specs=[ANY] * 4,
        out_specs=VMEM,
        scratch_shapes=[
            pltpu.VMEM((PARTS, TOK, 256), BF16),
            pltpu.VMEM((PARTS * 256, D), BF16),
            pltpu.VMEM((D, KMER * HD), BF16),
            pltpu.VMEM((TOK, D), BF16),
            pltpu.SemaphoreType.DMA((16,)),
            *gather_sems(3),
        ],
        compiler_params=pltpu.CompilerParams(
            collective_id=2, has_side_effects=True, vmem_limit_bytes=56 << 20
        ),
    )(att, tok, w_full, w_up)


def place_kernel(starts, lengths, expanded, w_class, own, lead, logits, wide, placed):
    for j in range(KMER):
        wide[pl.ds(j, TOK, stride=8), :] = expanded[:, j * HD : (j + 1) * HD].astype(F32)
    placed[:LEAD, :] = jnp.zeros((LEAD, HD), F32)
    placed[NUC:, :] = jnp.zeros((LEAD + 16, HD), F32)
    shift = LEAD - lax.axis_index("seq") * NUC

    def one(t, carry):
        placed[pl.ds(starts[t] + shift, 8), :] = wide[pl.ds(pl.multiple_of(t * 8, 8), 8), :]
        return carry

    lax.fori_loop(0, TOK, one, 0, unroll=8)
    end = starts[TOK - 1] + lengths[TOK - 1] + shift
    placed[pl.ds(end, 8), :] = jnp.zeros((8, HD), F32)
    lead[...] = placed[:LEAD, :].astype(BF16)
    rows = placed[LEAD : LEAD + NUC, :].astype(BF16)
    own[...] = rows
    logits[:, :NUC] = lax.dot_general(w_class[...], rows, NT, preferred_element_type=F32)
    logits[:, NUC:] = jnp.zeros((16, PARTS * PIECE - NUC), F32)


def place(starts, lengths, expanded, w_class):
    return pl.pallas_call(
        place_kernel,
        out_shape=(
            jax.ShapeDtypeStruct((NUC, HD), BF16),
            jax.ShapeDtypeStruct((LEAD, HD), BF16),
            jax.ShapeDtypeStruct((16, PARTS * PIECE), F32),
        ),
        in_specs=[SMEM, SMEM, VMEM, VMEM],
        out_specs=(VMEM, VMEM, VMEM),
        scratch_shapes=[
            pltpu.VMEM((TOK * 8, HD), F32),
            pltpu.VMEM((LEAD + NUC + 16, HD), F32),
        ],
        compiler_params=pltpu.CompilerParams(vmem_limit_bytes=48 << 20),
    )(starts, lengths, expanded, w_class)


def loss_kernel(
    lead, logits, w_class, labels, arriving, loss,
    pieces, received, lab, mine, lead_ss, lead_rs, p_ss, p_rs, a_ss, a_rs, lab_sem,
):
    seq = lax.axis_index("seq")
    mp = lax.axis_index("mp")
    before = {"seq": (seq + 15) % 16, "mp": mp}
    after = {"seq": (seq + 1) % 16, "mp": mp}
    others = [{"seq": seq, "mp": (mp + d) % PARTS} for d in range(1, PARTS)]
    head = 384
    lab_head = pltpu.make_async_copy(
        labels.at[pl.ds(mp * PIECE, head)], lab.at[pl.ds(0, head)], lab_sem.at[0]
    )
    lab_tail = pltpu.make_async_copy(
        labels.at[pl.ds(jnp.minimum(mp, PARTS - 2) * PIECE + head, PIECE - head)],
        lab.at[pl.ds(head, PIECE - head)], lab_sem.at[1],
    )
    lab_head.start()
    lab_tail.start()
    greet([before, after] + others)
    shift = remote(lead, arriving, lead_ss, lead_rs, before)
    shift.start()

    def piece(j):
        return logits[:, j * PIECE : (j + 1) * PIECE].astype(BF16)

    def copies(d):
        return remote(
            pieces.at[(mp + d) % PARTS], received.at[d - 1], p_ss.at[d - 1], p_rs.at[d - 1], others[d - 1]
        )

    for j in range(6):
        pieces[j] = piece(j)
    shift.wait_recv()
    late = NUC - LEAD
    logits[:, late:NUC] = logits[:, late:NUC] + lax.dot_general(
        w_class[...], arriving[...], NT, preferred_element_type=F32
    )
    for j in range(6, PARTS):
        pieces[j] = piece(j)
    for d in range(1, PARTS):
        copies(d).start()
    lab_head.wait()
    lab_tail.wait()
    picked = (
        lax.broadcasted_iota(jnp.int32, (16, CLASSES), 0) == lax.broadcasted_iota(jnp.int32, (16, CLASSES), 1)
    ).astype(BF16)
    marks = lax.dot_general(picked, lab[...].astype(BF16), NT, preferred_element_type=F32)
    for d in range(1, PARTS):
        copies(d).wait_recv()
    total = pieces[mp].astype(F32)
    for d in range(1, PARTS):
        total = total + received[d - 1].astype(F32)
    softplus = jnp.maximum(total, 0.0) + jnp.log(1.0 + jnp.exp(-jnp.abs(total)))
    terms = softplus - marks * total
    real = lax.broadcasted_iota(jnp.int32, terms.shape, 0) < CLASSES
    summed = jnp.sum(jnp.where(real, terms, 0.0), axis=0, keepdims=True)
    mine[...] = jnp.broadcast_to(summed, (8, PIECE))

    def spread(d):
        return remote(mine, loss.at[mp], a_ss.at[d - 1], a_rs.at[d - 1], others[d - 1])

    for d in range(1, PARTS):
        spread(d).start()
    loss[mp] = mine[...]
    for d in range(1, PARTS):
        spread(d).wait_recv()
    shift.wait_send()
    for d in range(1, PARTS):
        copies(d).wait_send()
        spread(d).wait_send()


def losses(lead, logits, w_class, labels):
    dma = pltpu.SemaphoreType.DMA
    return pl.pallas_call(
        loss_kernel,
        out_shape=(
            jax.ShapeDtypeStruct((LEAD, HD), BF16),
            jax.ShapeDtypeStruct((PARTS, 8, PIECE), F32),
        ),
        in_specs=[VMEM, VMEM, VMEM, ANY],
        out_specs=(VMEM, VMEM),
        scratch_shapes=[
            pltpu.VMEM((PARTS, 16, PIECE), BF16),
            pltpu.VMEM((PARTS - 1, 16, PIECE), BF16),
            pltpu.VMEM((PIECE, CLASSES), jnp.int32),
            pltpu.VMEM((8, PIECE), F32),
            dma, dma, dma((7,)), dma((7,)), dma((7,)), dma((7,)), dma((2,)),
        ],
        compiler_params=pltpu.CompilerParams(
            collective_id=3, has_side_effects=True, vmem_limit_bytes=32 << 20
        ),
    )(lead, logits, w_class, labels)


def per_device(
    tokens, norm_gain, w_query, w_key, w_value, w_out, w_up, w_class, starts, lengths, labels
):
    class_rows = jnp.pad(w_class.T, ((0, 2), (0, 0)))
    tok_full, q, k, v = project(tokens, norm_gain.reshape(1, D), w_query, w_key, w_value)
    att, w_full = attend(q, k, v, w_out)
    expanded = expand(att, tok_full, w_full, w_up)
    own, lead, logits = place(starts, lengths, expanded, class_rows)
    arriving, loss = losses(lead, logits, class_rows, labels)
    features = own.at[NUC - LEAD :].add(arriving)
    return (features, loss[:, 0, :].reshape(-1)[:NUC])


def solution(mesh):
    return jax.shard_map(
        per_device,
        mesh=mesh,
        in_specs=(
            P("seq", "mp"),
            P(),
            P(None, "mp"),
            P(None, "mp"),
            P(None, "mp"),
            P("mp", None),
            P(None, None, "mp"),
            P("mp", None),
            P("seq"),
            P("seq"),
            P("seq", None),
        ),
        out_specs=(P("seq", "mp"), P("seq")),
        check_vma=False,
    )
```

time: 564 us -> 152 us (0.27)
  waiting for transfers between devices: 288 us -> 0 us
  Pallas kernels: 0 us -> 143 us
  matrix products: 127 us -> 0 us
  other arithmetic: 71.5 us -> 1.63 us
  local copies, waits for them, and re-layouts: 56.8 us -> 5.96 us
  between operations: 14 us -> 0.74 us
    all_gather x3 -> x0, waiting for transfers between devices: 152 us -> none  [the longest x1 63.2 us: per_device(): value_piece = lax.all_gather(values, 'seq', axis=0, tiled=True)]
    pallas_call x0 -> x5, Pallas kernels: none -> 143 us  [the longest x1 56.4 us: attend(): pl.pallas_call(attend_kernel, out_shape=(jax.ShapeDtypeStruct((TOK, 256),...]
    psum x2 -> x0, waiting for transfers between devices: 130 us -> none  [the longest x1 68.7 us: per_device(): lax.psum(partial_value.astype(jnp.bfloat16), 'mp').astype(jnp.float32)]
    dot_general x30 -> x0, matrix products: 127 us -> none  [the longest x12 54 us: attend_block(): jnp.einsum('htr,rhd->htd', expos.astype(jnp.bfloat16), value_heads, prefe...]
    reduce_sum x15 -> x0, other arithmetic: 50.9 us -> none  [the longest x12 45.8 us: attend_block(): new_total = running_total * factor + jnp.sum(expos, axis=-1)]
    dynamic_slice x36 -> x0, local copies, waits for them, and re-layouts: 20.2 us -> none  [the longest x24 17.7 us: one_block(): lax.dynamic_slice_in_dim(value_piece, block_index * block_rows, block_row...]
    while x133 -> x0, local copies, waits for them, and re-layouts: 18.9 us -> none
    scatter x1 -> x0, local copies, waits for them, and re-layouts: 12.8 us -> none  [per_device(): placed = jnp.zeros((lead_rows + nuc_rows, local_channels), jnp.bfloat16)....]
  transfers between devices with their start and end apart: 6 -> 0, of which waited for: 6 -> 0; matrix products, arithmetic and copies ran while one was open for 2% -> 0% of each run, Pallas kernels for 0% -> 0%
where the time goes in v1:
time: 152 us; the launch traced here: 151 us
  Pallas kernels  143 us (94%)
  local copies, waits for them, and re-layouts  5.96 us (4%)
  other arithmetic  1.63 us (1%)
    pallas_call x1, Pallas kernels, attend(): pl.pallas_call(attend_kernel, out_shape=(jax.ShapeDtypeStruct((TOK, 256),...  56.4 us
    pallas_call x1, Pallas kernels, project(): pl.pallas_call(qkv_kernel, out_shape=(jax.ShapeDtypeStruct((TOK, D), BF16...  35.2 us
    pallas_call x1, Pallas kernels, expand(): pl.pallas_call(expand_kernel, out_shape=jax.ShapeDtypeStruct((TOK, KMER *...  33.2 us
    pallas_call x1, Pallas kernels, losses(): pl.pallas_call(loss_kernel, out_shape=(jax.ShapeDtypeStruct((LEAD, HD), B...  14.5 us
    unnamed x12, local copies, waits for them, and re-layouts  4.03 us
    pallas_call x1, Pallas kernels, place(): pl.pallas_call(place_kernel, out_shape=(jax.ShapeDtypeStruct((NUC, HD), B...  3.83 us

profile of v1, /device:TPU:1, one launch (start us, length us, event | category | flops | bytes accessed | tf_op | source)
XLA Modules:
  0.0 151.4 jit_solution(3791833339626194689)
XLA Ops:
  0.6 2.1 %copy.13.tokens = bf16[768,320]{1,0:T(8,128)(2,1)} copy(bf16[768,320]{0,1:T(8,128)(2,1)} %param.13) | data formatting | bytes 983040 | tf_op args[0]
  2.7 1.3 reshape.33.gain
  4.0 35.2 %shard_map.122 = (bf16[768,2560]{1,0:T(8,128)(2,1)}, bf16[256,768]{1,0:T(8,128)(2,1)}, bf16[2,768,128]{2,1,0:T(8,128)(2,1)}, bf16[256,768]{1,0:T(8,128)(2,1)}) custom-call(bf16[768,320]{1,0:T(8,128)(2,1)} %copy.13.tokens, f32[1,2560]{1,0:T(1,128)} %reshape.33.gain, bf16[2560,256]{1,0:T(8,128)(2,1)} %w_query.1, bf16[2560,256]{1,0:T(8,128)(2,1)} %w_key.1, ...), custom_call_target="tpu_custom_call" | custom-call | tf_op jit(solution)/shard_map/pallas_call | solution.py:193
  39.2 56.4 %shard_map.123 = (bf16[768,256]{1,0:T(8,128)(2,1)}, bf16[8,256,2560]{2,1,0:T(8,128)(2,1)}) custom-call(bf16[256,768]{1,0:T(8,128)(2,1)} %get-tuple-element.25.q_in, bf16[2,768,128]{2,1,0:T(8,128)(2,1)} %get-tuple-element.26.k_in, bf16[256,768]{1,0:T(8,128)(2,1)} %get-tuple-element.27.v_in, bf16[256,2560]{1,0:T(8,128)(2,1)} %w_out.1), custom_call_target="tpu_custom_call" | custom-call | tf_op jit(solution)/shard_map/pallas_call | solution.py:358
  95.6 0.0 copy-start.4
  95.6 0.0 copy-start.1
  95.6 0.0 copy-start.2
  95.6 0.0 copy-start.3
  95.6 33.2 %shard_map.124.expanded = bf16[768,768]{1,0:T(8,128)(2,1)} custom-call(bf16[768,256]{1,0:T(8,128)(2,1)} %get-tuple-element.28.att, bf16[768,2560]{1,0:T(8,128)(2,1)} %get-tuple-element.29.tok, bf16[8,256,2560]{2,1,0:T(8,128)(2,1)} %get-tuple-element.30.w_full, bf16[6,2560,128]{2,1,0:T(8,128)(2,1)} %w_up.1), custom_call_target="tpu_custom_call" | custom-call | tf_op jit(solution)/shard_map/pallas_call | solution.py:427
  128.8 0.0 copy-done.4
  128.9 0.0 copy-done.1
  128.9 0.0 copy-done.2
  128.9 0.0 copy-start
  128.9 1.3 copy-done
  130.2 3.8 %shard_map.125 = (bf16[3968,128]{1,0:T(8,128)(2,1)}, bf16[640,128]{1,0:T(8,128)(2,1)S(1)}, f32[16,4096]{1,0:T(8,128)S(1)}) custom-call(s32[768]{0:T(1024)S(1)} %copy-done.1, s32[768]{0:T(1024)S(1)} %copy-done.2, bf16[768,768]{1,0:T(8,128)(2,1)S(1)} %copy-done, bf16[16,128]{1,0:T(8,128)(2,1)S(1)} %pad.6.w_class), custom_call_target="tpu_custom_call" | custom-call | tf_op jit(solution)/shard_map/pallas_call | solution.py:468
  134.0 0.0 copy-done.3
  134.0 0.7 copy.14.labels
  134.7 14.5 %shard_map.126 = (bf16[640,128]{1,0:T(8,128)(2,1)S(1)}, f32[8,8,512]{2,1,0:T(8,128)S(1)}) custom-call(bf16[640,128]{1,0:T(8,128)(2,1)S(1)} %get-tuple-element.32.lead, f32[16,4096]{1,0:T(8,128)S(1)} %get-tuple-element.33.logits, bf16[16,128]{1,0:T(8,128)(2,1)S(1)} %pad.6.w_class, s32[3968,14]{1,0:T(8,128)S(1)} %copy.14.labels), custom_call_target="tpu_custom_call" | custom-call | tf_op jit(solution)/shard_map/pallas_call | solution.py:560
  149.2 1.6 %add_dynamic-update-slice_fusion = bf16[3968,128]{1,0:T(8,128)(2,1)} fusion(bf16[3968,128]{1,0:T(8,128)(2,1)} %get-tuple-element.31, bf16[640,128]{1,0:T(8,128)(2,1)S(1)} %get-tuple-element.34), kind=kLoop, calls=%fused_computation | loop fusion | flops 327680 | bytes 491520 | tf_op jit(solution)/shard_map/scatter-add | solution.py:590
  150.8 0.6 slice.26
  (1 shorter events, 0.0 us)
Async XLA Ops:
  95.6 33.3 %copy-start.4 = (bf16[128,14]{0,1:T(8,128)(2,1)S(1)}, bf16[128,14]{0,1:T(8,128)(2,1)}, u32[]{:S(2)}) copy-start(bf16[128,14]{0,1:T(8,128)(2,1)} %param.20) | copy-start | bytes 10756
  95.6 33.3 %copy-start.1 = (s32[768]{0:T(1024)S(1)}, s32[768]{0:T(1024)}, u32[]{:S(2)}) copy-start(s32[768]{0:T(1024)} %starts.1) | copy-start | bytes 9220
  95.6 33.3 %copy-start.2 = (s32[768]{0:T(1024)S(1)}, s32[768]{0:T(1024)}, u32[]{:S(2)}) copy-start(s32[768]{0:T(1024)} %lengths.1) | copy-start | bytes 9220
  95.6 38.4 %copy-start.3 = (s32[3968,14]{0,1:T(8,128)S(1)}, s32[3968,14]{0,1:T(8,128)}, u32[]{:S(2)}) copy-start(s32[3968,14]{0,1:T(8,128)} %param.23) | copy-start | bytes 666628
  128.9 1.3 copy-start

commit v2 on v1

v2 whole, which is shorter than its diff:
```python
import functools
import math

import jax
import jax.numpy as jnp
from jax import lax
from jax.experimental import pallas as pl
from jax.experimental.pallas import tpu as pltpu
from jax.sharding import PartitionSpec as P

HD = 128
KMER = 6
TOK = 768
D = 2560
NUC = 3968
LEAD = 640
PIECE = 512
PARTS = 8
CLASSES = 14
MESH = pl.DeviceIdType.MESH
ANY = pl.BlockSpec(memory_space=pl.ANY)
VMEM = pl.BlockSpec(memory_space=pltpu.VMEM)
SMEM = pl.BlockSpec(memory_space=pltpu.SMEM)
BF16 = jnp.bfloat16
F32 = jnp.float32
NT = (((1,), (1,)), ((), ()))


def coords():
    seq = lax.axis_index("seq")
    mp = lax.axis_index("mp")
    return seq // 4, mp // 2, seq % 4, mp % 2


def device(x, y, z, core):
    return {"seq": x * 4 + z, "mp": y * 2 + core}


def greet(partners):
    barrier = pltpu.get_barrier_semaphore()
    for partner in partners:
        pl.semaphore_signal(barrier, inc=1, device_id=partner, device_id_type=MESH)
    pl.semaphore_wait(barrier, len(partners))


def remote(src, dst, send_sem, recv_sem, target):
    return pltpu.make_async_remote_copy(
        src_ref=src, dst_ref=dst, send_sem=send_sem, recv_sem=recv_sem, device_id=target, device_id_type=MESH
    )


class Gather:
    def __init__(self, src, buf, extent, chunks, y_send, y_recv, f_send, f_recv, c_send, c_recv, wide=0):
        self.src, self.buf, self.step, self.wide = src, buf, extent // chunks, wide
        self.chunks = chunks
        self.sems = (y_send, y_recv, f_send, f_recv, c_send, c_recv)
        x, y, z, core = coords()
        up, down, far = (y + 1) % 4, (y + 3) % 4, (y + 2) % 4
        self.up, self.down = device(x, up, z, core), device(x, down, z, core)
        self.sibling = device(x, y, z, 1 - core)
        self.own = y * 2 + core
        self.slots = [y * 2 + core, down * 2 + core, up * 2 + core, far * 2 + core]
        self.twins = [y * 2 + 1 - core, down * 2 + 1 - core, up * 2 + 1 - core, far * 2 + 1 - core]

    def partners(self):
        return [self.up, self.down, self.sibling]

    def cut(self, r, part):
        if part is None:
            return pl.ds(r * self.step, self.step)
        half = self.step // 2
        return pl.ds(r * self.step + part * half, half)

    def mine(self, r):
        cut = self.cut(r, None)
        return self.src.at[:, cut] if self.wide else self.src.at[cut]

    def at(self, slot, r, part=None):
        cut = self.cut(r, part)
        if self.wide:
            return self.buf.at[pl.ds(pl.multiple_of(slot * self.wide, 16), self.wide), cut]
        return self.buf.at[slot, cut]

    def toward(self, way):
        return self.up if way == 0 else self.down

    def around(self, way, r):
        y_send, y_recv = self.sems[:2]
        return remote(self.mine(r), self.at(self.own, r), y_send.at[way, r], y_recv.at[way, r], self.toward(way))

    def arrived(self, way, r):
        y_send, y_recv = self.sems[:2]
        slot = self.at(self.slots[1 + way], r)
        return remote(slot, slot, y_send.at[way, r], y_recv.at[way, r], self.toward(way))

    def onward(self, way, r):
        f_send, f_recv = self.sems[2:4]
        slot = self.at(self.slots[1 + way], r, way)
        return remote(slot, slot, f_send.at[way, r], f_recv.at[way, r], self.toward(way))

    def far_arrived(self, way, r):
        f_send, f_recv = self.sems[2:4]
        slot = self.at(self.slots[3], r, way)
        return remote(slot, slot, f_send.at[way, r], f_recv.at[way, r], self.toward(way))

    def across(self, which, r, arriving=False):
        c_send, c_recv = self.sems[4:]
        part = which - 3 if which >= 3 else None
        slots = self.twins if arriving else self.slots
        slot = self.at(slots[min(which, 3)], r, part)
        src = self.mine(r) if which == 0 and not arriving else slot
        return remote(src, slot, c_send.at[which, r], c_recv.at[which, r], self.sibling)

    def start(self, first=0, last=None):
        for r in range(first, self.chunks if last is None else last):
            self.around(0, r).start()
            self.around(1, r).start()
            self.across(0, r).start()

    def forward(self, r):
        for way in range(2):
            self.arrived(way, r).wait_recv()
            self.onward(way, r).start()
            self.across(1 + way, r).start()

    def forward_far(self, r):
        for way in range(2):
            self.far_arrived(way, r).wait_recv()
            self.across(3 + way, r).start()

    def complete(self, r):
        for which in range(5):
            self.across(which, r, arriving=True).wait_recv()

    def sent(self):
        for r in range(self.chunks):
            for way in range(2):
                self.around(way, r).wait_send()
                self.onward(way, r).wait_send()
            for which in range(5):
                self.across(which, r).wait_send()


def gather_sems(chunks):
    dma = pltpu.SemaphoreType.DMA
    return [dma((2, chunks)), dma((2, chunks)), dma((2, chunks)), dma((2, chunks)), dma((5, chunks)), dma((5, chunks))]


def pick(index, options):
    value = options[-1]
    for i in range(len(options) - 2, -1, -1):
        value = jnp.where(index == i, options[i], value)
    return value


CHUNKS = 3
STEP = TOK // CHUNKS
PARTS_W = 4
UNITS = [
    (0, 0), (1, 0), (2, 0), (1, 1), (2, 1), (1, 2), (2, 2), (0, 1),
    (3, 0), (3, 1), (3, 2), (3, 3), (1, 3), (2, 3), (0, 2), (0, 3),
]


def attend_kernel(
    tokens, gain, w_query, w_key, w_value, w_out, w_up, att, w_full, base,
    xb, weights, turned, up_in, up_turned, gains, qb, kb, vb, acc, top, o_send, l_send, o_recv, l_recv,
    local, q_ss, q_rs, k_ss, k_rs, v_ss, v_rs, o_ss, o_rs, l_ss, l_rs, *sems,
):
    x, y, z, core = coords()
    tok_ring = Gather(tokens, xb, TOK, CHUNKS, *sems[:6], wide=D // PARTS)
    ring = Gather(w_out, w_full, 256, PARTS_W, *sems[6:])

    def along(axis, by):
        if axis == 0:
            return device((x + by + 4) % 4, y, z, core)
        return device(x, y, (z + by + 4) % 4, core)

    offsets = {1: 1, 2: -1, 3: 2}

    def move(kind, h, slot, r):
        target = along(1 - h if kind == "q" else h, -offsets[slot])
        part = pl.ds(r * STEP, STEP)
        if kind == "q":
            src, dst, ss, rs = qb.at[h, 0, :, part], qb.at[h, slot, :, part], q_ss, q_rs
        elif kind == "k":
            src, dst, ss, rs = kb.at[h, 0, part], kb.at[h, slot, part], k_ss, k_rs
        else:
            src, dst, ss, rs = vb.at[h, 0, :, part], vb.at[h, slot, :, part], v_ss, v_rs
        return remote(src, dst, ss.at[h, slot, r], rs.at[h, slot, r], target)

    def send(slots, r):
        for kind in "qkv":
            for slot in slots:
                for h in range(2):
                    move(kind, h, slot, r).start()

    def lift(r):
        cut = pl.ds(r * STEP, STEP)
        base[cut, :] = jnp.dot(up_turned[...], xb[:, cut], preferred_element_type=F32).T

    own = pltpu.make_async_copy(
        tokens, xb.at[pl.ds(pl.multiple_of(tok_ring.own * (D // PARTS), 16), D // PARTS)], local.at[0]
    )
    own.start()
    loads = [pltpu.make_async_copy(w, weights.at[i], local.at[1 + i]) for i, w in enumerate((w_query, w_key, w_value))]
    for load in loads:
        load.start()
    own_w = pltpu.make_async_copy(w_out, w_full.at[ring.own], local.at[4])
    own_w.start()
    ups = [pltpu.make_async_copy(w_up.at[j], up_in.at[:, pl.ds(j * HD, HD)], local.at[5 + j]) for j in range(KMER)]
    for load in ups:
        load.start()
    greet([along(a, by) for a in range(2) for by in (1, -1, 2)] + ring.partners())
    tok_ring.start(0, 1)
    for i in range(D // HD):
        gains[pl.ds(i * HD, HD), :] = jnp.broadcast_to(gain[pl.ds(i, 1), :], (HD, HD)).T

    def turn(i):
        loads[i].wait()
        for j in range(D // 256):
            turned[pl.ds(i * 256, 256), pl.ds(j * 256, 256)] = weights[i, pl.ds(j * 256, 256), :].T

    def turn_up(i):
        for j in range(D // 256):
            up_turned[pl.ds(i * 256, 256), pl.ds(j * 256, 256)] = up_in[pl.ds(j * 256, 256), pl.ds(i * 256, 256)].T

    scale = math.log2(math.e) / math.sqrt(HD)

    def heads(r):
        tok_ring.complete(r)
        cut = pl.ds(r * STEP, STEP)
        wide = xb[:, cut].astype(F32)
        centred = wide - jnp.mean(wide, axis=0, keepdims=True)
        variance = jnp.mean(centred * centred, axis=0, keepdims=True)
        column = jnp.concatenate([gains[...]] * (STEP // HD), axis=1)
        normed = (centred * lax.rsqrt(variance + 1e-05) * column).astype(BF16)
        qkv = jnp.dot(turned[...], normed, preferred_element_type=F32)
        for h in range(2):
            at = h * HD
            qb[h, 0, :, cut] = (qkv[at : at + HD] * scale).astype(BF16)
            kb[h, 0, cut, :] = qkv[256 + at : 256 + at + HD].T.astype(BF16)
            vb[h, 0, :, cut] = qkv[512 + at : 512 + at + HD].astype(BF16)
        send((1, 2), r)

    turn(0)
    tok_ring.start(1, 2)
    turn(1)
    turn(2)
    own.wait()
    tok_ring.forward(0)
    tok_ring.start(2, 3)
    for load in ups:
        load.wait()
    turn_up(0)
    top[...] = jnp.full(top.shape, -1e30, F32)
    acc[...] = jnp.zeros(acc.shape, F32)
    tok_ring.forward(1)
    tok_ring.forward_far(0)
    turn_up(1)
    heads(0)
    tok_ring.forward(2)
    tok_ring.forward_far(1)
    ring.start()
    heads(1)
    tok_ring.forward_far(2)
    turn_up(2)
    heads(2)

    ones = jnp.ones((16, TOK), BF16)

    def partial(h, a):
        total = acc[h, a, HD : HD + 8, :]
        return acc[h, a, :HD, :] / total[:1], top[h, a] + jnp.log2(total)

    def give(h, slot):
        by = pick(slot - 1, [1, -1, 2])
        target = along(1 - h, by)
        return [
            remote(o_send.at[h, slot - 1], o_recv.at[h, slot - 1], o_ss.at[h, slot - 1], o_rs.at[h, slot - 1], target),
            remote(l_send.at[h, slot - 1], l_recv.at[h, slot - 1], l_ss.at[h, slot - 1], l_rs.at[h, slot - 1], target),
        ]

    def unit(i, carry):
        def arrivals(kinds, slot):
            for kind in kinds:
                for h in range(2):
                    for r in range(CHUNKS):
                        move(kind, h, slot, r).wait_recv()

        @pl.when(i == 1)
        def _():
            for r in range(CHUNKS):
                send((3,), r)
            lift(0)
            lift(1)

        for index, kinds, slot in ((1, "q", 1), (2, "q", 2), (3, "kv", 1), (5, "kv", 2), (8, "q", 3), (11, "kv", 3)):
            pl.when(i == index)(functools.partial(arrivals, kinds, slot))
        for r, index in enumerate((2, 5, 9, 12)):
            pl.when(i == index)(functools.partial(ring.forward, r))
        a = pick(i, [u[0] for u in UNITS])
        b = pick(i, [u[1] for u in UNITS])
        scores = [
            jnp.dot(kb[h, b], qb[h, a], preferred_element_type=F32) for h in range(2)
        ]
        for h in range(2):
            s = scores[h]
            before = top[h, a]
            now = jnp.maximum(before, jnp.max(s, axis=0, keepdims=True))
            weights = jnp.exp2(s - now[:1]).astype(BF16)
            factor = jnp.exp2(before - now)
            lhs = jnp.concatenate([vb[h, b], ones], axis=0)
            added = jnp.dot(lhs, weights, preferred_element_type=F32)
            acc[h, a] = acc[h, a] * factor[:1] + added
            top[h, a] = now

        @pl.when(jnp.logical_and(i >= 11, i < 14))
        def _():
            for h in range(2):
                value, level = partial(h, a)
                o_send[h, a - 1] = value.astype(BF16)
                l_send[h, a - 1] = level
                for copy in give(h, a):
                    copy.start()

        return carry

    lax.fori_loop(0, len(UNITS), unit, 0)
    lift(CHUNKS - 1)
    for r in range(PARTS_W):
        ring.forward_far(r)
    for h in range(2):
        value, level = partial(h, 0)
        for slot in range(1, 4):
            for copy in give(h, slot):
                copy.wait_recv()
        levels = [level] + [l_recv[h, i] for i in range(3)]
        highest = functools.reduce(jnp.maximum, levels)
        shares = [jnp.exp2(one - highest) for one in levels]
        total = functools.reduce(jnp.add, shares)
        shares = [share / total for share in shares]
        value = value * shares[0][:1]
        for i in range(3):
            value = value + o_recv[h, i].astype(F32) * shares[1 + i][:1]
        att[:, pl.ds(h * HD, HD)] = value.T.astype(BF16)
    own_w.wait()
    for r in range(PARTS_W):
        ring.complete(r)
    tok_ring.sent()
    ring.sent()
    for h in range(2):
        for slot in range(1, 4):
            for kind in "qkv":
                for r in range(CHUNKS):
                    move(kind, h, slot, r).wait_send()
            for copy in give(h, slot):
                copy.wait_send()


def attend(tokens, gain, w_query, w_key, w_value, w_out, w_up):
    dma = pltpu.SemaphoreType.DMA
    return pl.pallas_call(
        attend_kernel,
        out_shape=(
            jax.ShapeDtypeStruct((TOK, 256), BF16),
            jax.ShapeDtypeStruct((PARTS, 256, D), BF16),
            jax.ShapeDtypeStruct((TOK, KMER * HD), F32),
        ),
        in_specs=[ANY, VMEM, ANY, ANY, ANY, ANY, ANY],
        out_specs=(VMEM, ANY, VMEM),
        scratch_shapes=[
            pltpu.VMEM((D, TOK), BF16),
            pltpu.VMEM((3, D, 256), BF16),
            pltpu.VMEM((768, D), BF16),
            pltpu.VMEM((D, KMER * HD), BF16),
            pltpu.VMEM((KMER * HD, D), BF16),
            pltpu.VMEM((D, HD), F32),
            pltpu.VMEM((2, 4, HD, TOK), BF16),
            pltpu.VMEM((2, 4, TOK, HD), BF16),
            pltpu.VMEM((2, 4, HD, TOK), BF16),
            pltpu.VMEM((2, 4, HD + 16, TOK), F32),
            pltpu.VMEM((2, 4, 8, TOK), F32),
            pltpu.VMEM((2, 3, HD, TOK), BF16),
            pltpu.VMEM((2, 3, 8, TOK), F32),
            pltpu.VMEM((2, 3, HD, TOK), BF16),
            pltpu.VMEM((2, 3, 8, TOK), F32),
            dma((5 + KMER,)),
            *[dma((2, 4, CHUNKS)) for _ in range(6)],
            *[dma((2, 3)) for _ in range(4)],
            *gather_sems(CHUNKS),
            *gather_sems(PARTS_W),
        ],
        compiler_params=pltpu.CompilerParams(
            collective_id=0, has_side_effects=True, vmem_limit_bytes=56 << 20
        ),
    )(tokens, gain, w_query, w_key, w_value, w_out, w_up)


def gelu(x):
    return 0.5 * x * (1.0 + jnp.tanh(math.sqrt(2.0 / math.pi) * (x + 0.044715 * x * x * x)))


def expand_kernel(att, base, w_full, w_up, out, blocks, wo_v, wu_v, base_v, joint, local, *sems):
    ring = Gather(att, blocks, TOK, CHUNKS, *sems)
    ups = [pltpu.make_async_copy(w_up.at[j], wu_v.at[:, pl.ds(j * HD, HD)], local.at[2 + j]) for j in range(KMER)]
    outs = [pltpu.make_async_copy(w_full.at[j], wo_v.at[j], local.at[8 + j]) for j in range(PARTS)]
    lifted = pltpu.make_async_copy(base, base_v, local.at[1])
    own = pltpu.make_async_copy(att, blocks.at[ring.own], local.at[0])
    for load in [*ups, *outs, own, lifted]:
        load.start()
    greet(ring.partners())
    ring.start(0, 1)
    for load in ups:
        load.wait()

    def merge(i):
        outs[i].wait()
        joint[pl.ds(i * 256, 256), :] = jnp.dot(wo_v[i], wu_v[...], preferred_element_type=F32).astype(BF16)

    def finish(r):
        ring.complete(r)
        cut = pl.ds(r * STEP, STEP)
        joined = jnp.concatenate([blocks[j, cut, :] for j in range(PARTS)], axis=1)
        raised = base_v[cut, :] + jnp.dot(joined, joint[...], preferred_element_type=F32)
        out[cut, :] = gelu(raised).astype(BF16)

    merge(0)
    merge(1)
    ring.start(1, 2)
    merge(2)
    merge(3)
    ring.forward(0)
    merge(4)
    ring.start(2, 3)
    merge(5)
    merge(6)
    ring.forward(1)
    ring.forward_far(0)
    merge(7)
    own.wait()
    lifted.wait()
    ring.forward(2)
    ring.forward_far(1)
    finish(0)
    ring.forward_far(2)
    finish(1)
    finish(2)
    ring.sent()


def expand(att, base, w_full, w_up):
    return pl.pallas_call(
        expand_kernel,
        out_shape=jax.ShapeDtypeStruct((TOK, KMER * HD), BF16),
        in_specs=[ANY] * 4,
        out_specs=VMEM,
        scratch_shapes=[
            pltpu.VMEM((PARTS, TOK, 256), BF16),
            pltpu.VMEM((PARTS, 256, D), BF16),
            pltpu.VMEM((D, KMER * HD), BF16),
            pltpu.VMEM((TOK, KMER * HD), F32),
            pltpu.VMEM((PARTS * 256, KMER * HD), BF16),
            pltpu.SemaphoreType.DMA((16,)),
            *gather_sems(CHUNKS),
        ],
        compiler_params=pltpu.CompilerParams(
            collective_id=2, has_side_effects=True, vmem_limit_bytes=56 << 20
        ),
    )(att, base, w_full, w_up)


def place_kernel(starts, lengths, expanded, w_class, own, lead, logits, lead_logits, wide, placed, classes):
    for j in range(KMER):
        wide[pl.ds(j, TOK, stride=8), :] = expanded[:, j * HD : (j + 1) * HD].astype(F32)
    placed[:LEAD, :] = jnp.zeros((LEAD, HD), F32)
    placed[NUC:, :] = jnp.zeros((LEAD + 16, HD), F32)
    classes[...] = jnp.zeros(classes.shape, F32)
    classes[:CLASSES, :] = w_class[...].astype(F32)
    shift = LEAD - lax.axis_index("seq") * NUC

    def one(t, carry):
        placed[pl.ds(starts[t] + shift, 8), :] = wide[pl.ds(pl.multiple_of(t * 8, 8), 8), :]
        return carry

    lax.fori_loop(0, TOK, one, 0, unroll=8)
    end = starts[TOK - 1] + lengths[TOK - 1] + shift
    placed[pl.ds(end, 8), :] = jnp.zeros((8, HD), F32)
    first = placed[:LEAD, :].astype(BF16)
    lead[...] = first
    rows = placed[LEAD : LEAD + NUC, :].astype(BF16)
    own[...] = rows
    spread = classes[...].astype(BF16)
    partial = lax.dot_general(spread, rows, NT, preferred_element_type=F32).astype(BF16)
    for j in range(PARTS - 1):
        logits[j] = partial[:, j * PIECE : (j + 1) * PIECE]
    rest = NUC - (PARTS - 1) * PIECE
    logits[PARTS - 1, :, :rest] = partial[:, (PARTS - 1) * PIECE :]
    logits[PARTS - 1, :, rest:] = jnp.zeros((16, PIECE - rest), BF16)
    lead_logits[...] = lax.dot_general(spread, first, NT, preferred_element_type=F32).astype(BF16)


def place(starts, lengths, expanded, w_class):
    return pl.pallas_call(
        place_kernel,
        out_shape=(
            jax.ShapeDtypeStruct((NUC, HD), BF16),
            jax.ShapeDtypeStruct((LEAD, HD), BF16),
            jax.ShapeDtypeStruct((PARTS, 16, PIECE), BF16),
            jax.ShapeDtypeStruct((16, LEAD), BF16),
        ),
        in_specs=[SMEM, SMEM, VMEM, VMEM],
        out_specs=(VMEM, VMEM, VMEM, VMEM),
        scratch_shapes=[
            pltpu.VMEM((TOK * 8, HD), F32),
            pltpu.VMEM((LEAD + NUC + 16, HD), F32),
            pltpu.VMEM((16, HD), F32),
        ],
        compiler_params=pltpu.CompilerParams(vmem_limit_bytes=48 << 20),
    )(starts, lengths, expanded, w_class)


def loss_kernel(
    lead, pieces, lead_logits, labels, arriving, loss,
    received, early, late, total, lab, mine, lead_ss, lead_rs, p_ss, p_rs, e_ss, e_rs, t_ss, t_rs, a_ss, a_rs, lab_sem,
):
    seq = lax.axis_index("seq")
    mp = lax.axis_index("mp")
    before, after = (seq + 15) % 16, (seq + 1) % 16
    others = [{"seq": seq, "mp": (mp + d) % PARTS} for d in range(1, PARTS)]
    head = NUC - (PARTS - 1) * PIECE
    split = (PARTS - 1) * PIECE - (NUC - LEAD)
    lab_head = pltpu.make_async_copy(
        labels.at[:, pl.ds(pl.multiple_of(mp * PIECE, PIECE), head)], lab.at[:, pl.ds(0, head)], lab_sem.at[0]
    )
    lab_tail = pltpu.make_async_copy(
        labels.at[:, pl.ds(pl.multiple_of(jnp.minimum(mp, PARTS - 2) * PIECE + head, HD), PIECE - head)],
        lab.at[:, pl.ds(head, PIECE - head)], lab_sem.at[1],
    )
    lab_head.start()
    lab_tail.start()

    barrier = pltpu.get_barrier_semaphore()
    for other in others + [{"seq": after, "mp": mp}]:
        pl.semaphore_signal(barrier, inc=1, device_id=other, device_id_type=MESH)

    @pl.when(mp >= PARTS - 2)
    def _():
        for j in range(PARTS):
            pl.semaphore_signal(barrier, inc=1, device_id={"seq": after, "mp": j}, device_id_type=MESH)

    pl.semaphore_wait(barrier, PARTS + 2)

    def piece(d):
        return remote(
            pieces.at[(mp + d) % PARTS], received.at[d - 1], p_ss.at[d - 1], p_rs.at[d - 1], others[d - 1]
        )

    def early_copy(slot):
        return remote(
            lead_logits.at[:, pl.ds(0, split)], early.at[slot], e_ss, e_rs.at[slot], {"seq": before, "mp": PARTS - 2}
        )

    def late_copy(slot):
        return remote(
            lead_logits.at[:, pl.ds(split, head)], late.at[slot], t_ss, t_rs.at[slot], {"seq": before, "mp": PARTS - 1}
        )

    early_copy(mp).start()
    late_copy(mp).start()
    for d in range(1, PARTS):
        piece(d).start()
    shift = remote(lead, arriving, lead_ss, lead_rs, {"seq": before, "mp": mp})
    shift.start()
    lab_head.wait()
    lab_tail.wait()
    for d in range(1, PARTS):
        piece(d).wait_recv()
    summed = pieces[mp].astype(F32)
    for d in range(1, PARTS):
        summed = summed + received[d - 1].astype(F32)
    total[...] = summed

    @pl.when(mp == PARTS - 2)
    def _():
        for j in range(PARTS):
            early_copy(j).wait_recv()
        for j in range(PARTS):
            total[:, PIECE - split :] = total[:, PIECE - split :] + early[j].astype(F32)

    @pl.when(mp == PARTS - 1)
    def _():
        for j in range(PARTS):
            late_copy(j).wait_recv()
        for j in range(PARTS):
            total[:, :head] = total[:, :head] + late[j].astype(F32)

    logit = total[:CLASSES, :]
    softplus = jnp.maximum(logit, 0.0) + jnp.log(1.0 + jnp.exp(-jnp.abs(logit)))
    terms = softplus - lab[...].astype(F32) * logit
    mine[...] = jnp.broadcast_to(jnp.sum(terms, axis=0, keepdims=True), (8, PIECE))

    def spread(d):
        return remote(mine, loss.at[mp], a_ss.at[d - 1], a_rs.at[d - 1], others[d - 1])

    for d in range(1, PARTS):
        spread(d).start()
    loss[mp] = mine[...]
    for d in range(1, PARTS):
        spread(d).wait_recv()
    shift.wait()
    early_copy(mp).wait_send()
    late_copy(mp).wait_send()
    for d in range(1, PARTS):
        piece(d).wait_send()
        spread(d).wait_send()


def losses(lead, pieces, lead_logits, labels):
    dma = pltpu.SemaphoreType.DMA
    head = NUC - (PARTS - 1) * PIECE
    return pl.pallas_call(
        loss_kernel,
        out_shape=(
            jax.ShapeDtypeStruct((LEAD, HD), BF16),
            jax.ShapeDtypeStruct((PARTS, 8, PIECE), F32),
        ),
        in_specs=[VMEM, VMEM, VMEM, ANY],
        out_specs=(VMEM, VMEM),
        scratch_shapes=[
            pltpu.VMEM((PARTS - 1, 16, PIECE), BF16),
            pltpu.VMEM((PARTS, 16, LEAD - head), BF16),
            pltpu.VMEM((PARTS, 16, head), BF16),
            pltpu.VMEM((16, PIECE), F32),
            pltpu.VMEM((CLASSES, PIECE), jnp.int32),
            pltpu.VMEM((8, PIECE), F32),
            dma, dma, dma((7,)), dma((7,)), dma, dma((PARTS,)), dma, dma((PARTS,)), dma((7,)), dma((7,)), dma((2,)),
        ],
        compiler_params=pltpu.CompilerParams(
            collective_id=3, has_side_effects=True, vmem_limit_bytes=32 << 20
        ),
    )(lead, pieces, lead_logits, labels)


def per_device(
    tokens, norm_gain, w_query, w_key, w_value, w_out, w_up, w_class, starts, lengths, labels
):
    att, w_full, base = attend(tokens.T, norm_gain.reshape(D // HD, HD), w_query, w_key, w_value, w_out, w_up)
    expanded = expand(att, base, w_full, w_up)
    own, lead, logits, lead_logits = place(starts, lengths, expanded, w_class.T)
    arriving, loss = losses(lead, logits, lead_logits, labels.T)
    features = own.at[NUC - LEAD :].add(arriving)
    return (features, loss[:, 0, :].reshape(-1)[:NUC])


def solution(mesh):
    return jax.shard_map(
        per_device,
        mesh=mesh,
        in_specs=(
            P("seq", "mp"),
            P(),
            P(None, "mp"),
            P(None, "mp"),
            P(None, "mp"),
            P("mp", None),
            P(None, None, "mp"),
            P("mp", None),
            P("seq"),
            P("seq"),
            P("seq", None),
        ),
        out_specs=(P("seq", "mp"), P("seq")),
        check_vma=False,
    )
```

time: 152 us -> 125 us (0.82)
  Pallas kernels: 143 us -> 121 us
  local copies, waits for them, and re-layouts: 5.96 us -> 1.9 us
    pallas_call x1 -> x0, Pallas kernels: 35.2 us -> none  [project(): pl.pallas_call(qkv_kernel, out_shape=(jax.ShapeDtypeStruct((TOK, D), BF16...]
    pallas_call x1, Pallas kernels: 56.4 us -> 82.9 us  [attend(): pl.pallas_call(attend_kernel, out_shape=(jax.ShapeDtypeStruct((TOK, 256),...]
    pallas_call x1, Pallas kernels: 33.2 us -> 22.3 us  [expand(): pl.pallas_call(expand_kernel, out_shape=jax.ShapeDtypeStruct((TOK, KMER *...]
    pallas_call x1, Pallas kernels: 14.5 us -> 11.8 us  [losses(): pl.pallas_call(loss_kernel, out_shape=(jax.ShapeDtypeStruct((LEAD, HD), B...]
    unnamed x12 -> x10, local copies, waits for them, and re-layouts: 4.03 us -> 1.29 us
where the time goes in v2:
time: 125 us
  Pallas kernels  121 us (97%)
  local copies, waits for them, and re-layouts  1.9 us (2%)
  other arithmetic  1.63 us (1%)
    pallas_call x1, Pallas kernels, attend(): pl.pallas_call(attend_kernel, out_shape=(jax.ShapeDtypeStruct((TOK, 256),...  82.9 us
    pallas_call x1, Pallas kernels, expand(): pl.pallas_call(expand_kernel, out_shape=jax.ShapeDtypeStruct((TOK, KMER *...  22.3 us
    pallas_call x1, Pallas kernels, losses(): pl.pallas_call(loss_kernel, out_shape=(jax.ShapeDtypeStruct((LEAD, HD), B...  11.8 us
    pallas_call x1, Pallas kernels, place(): pl.pallas_call(place_kernel, out_shape=(jax.ShapeDtypeStruct((NUC, HD), B...  3.77 us

profile of v2, /device:TPU:1, one launch (start us, length us, event | category | flops | bytes accessed | tf_op | source)
XLA Modules:
  0.0 125.0 jit_solution(17814113215104543019)
XLA Ops:
  0.6 82.9 %shard_map.122 = (bf16[768,256]{1,0:T(8,128)(2,1)}, bf16[8,256,2560]{2,1,0:T(8,128)(2,1)}, f32[768,768]{1,0:T(8,128)}) custom-call(bf16[320,768]{1,0:T(8,128)(2,1)} %bitcast.8, f32[20,128]{1,0:T(8,128)} %bitcast.10, bf16[2560,256]{1,0:T(8,128)(2,1)} %w_query.1, bf16[2560,256]{1,0:T(8,128)(2,1)} %w_key.1, bf16[2560,256]{1,0:T(8,128)(2,1)} %w_value.1, ...), custom_call_target="tpu_custom_call" | custom-call | tf_op jit(solution)/shard_map/pallas_call | solution.py:363
  83.5 0.0 copy-start.2
  83.5 0.0 copy-start.3
  83.5 0.0 copy-start.4
  83.6 22.3 %shard_map.123.expanded = bf16[768,768]{1,0:T(8,128)(2,1)} custom-call(bf16[768,256]{1,0:T(8,128)(2,1)} %get-tuple-element.23.att, f32[768,768]{1,0:T(8,128)} %get-tuple-element.24.base, bf16[8,256,2560]{2,1,0:T(8,128)(2,1)} %get-tuple-element.25.w_full, bf16[6,2560,128]{2,1,0:T(8,128)(2,1)} %w_up.3), custom_call_target="tpu_custom_call" | custom-call | tf_op jit(solution)/shard_map/pallas_call | solution.py:453
  105.9 0.0 copy-done.2
  105.9 0.0 copy-done.3
  105.9 0.0 copy-done.4
  105.9 0.0 copy-start
  105.9 1.3 %copy-done = bf16[768,768]{1,0:T(8,128)(2,1)S(1)} copy-done((bf16[768,768]{1,0:T(8,128)(2,1)S(1)}, bf16[768,768]{1,0:T(8,128)(2,1)}, u32[]{:S(2)}) %copy-start) | copy-done | bytes 1179672
  107.2 0.0 copy-start.1
  107.2 3.8 %shard_map.124 = (bf16[3968,128]{1,0:T(8,128)(2,1)}, bf16[640,128]{1,0:T(8,128)(2,1)S(1)}, bf16[8,16,512]{2,1,0:T(8,128)(2,1)S(1)}, bf16[16,640]{1,0:T(8,128)(2,1)S(1)}) custom-call(s32[768]{0:T(1024)S(1)} %copy-done.2, s32[768]{0:T(1024)S(1)} %copy-done.3, bf16[768,768]{1,0:T(8,128)(2,1)S(1)} %copy-done, bf16[14,128]{1,0:T(8,128)(2,1)S(1)} %bitcast.7), custom_call_target="tpu_custom_call" | custom-call | tf_op jit(solution)/shard_map/pallas_call | solution.py:504
  111.0 0.0 copy-done.1
  111.0 11.8 %shard_map.125 = (bf16[640,128]{1,0:T(8,128)(2,1)S(1)}, f32[8,8,512]{2,1,0:T(8,128)S(1)}) custom-call(bf16[640,128]{1,0:T(8,128)(2,1)S(1)} %get-tuple-element.27.lead, bf16[8,16,512]{2,1,0:T(8,128)(2,1)S(1)} %get-tuple-element.28.pieces, bf16[16,640]{1,0:T(8,128)(2,1)S(1)} %get-tuple-element.29.lead_logits, s32[14,3968]{1,0:T(8,128)S(1)} %bitcast.6), custom_call_target="tpu_custom_call" | custom-call | tf_op jit(solution)/shard_map/pallas_call | solution.py:622
  122.7 1.6 %add_dynamic-update-slice_fusion = bf16[3968,128]{1,0:T(8,128)(2,1)} fusion(bf16[3968,128]{1,0:T(8,128)(2,1)} %get-tuple-element.26, bf16[640,128]{1,0:T(8,128)(2,1)S(1)} %get-tuple-element.30), kind=kLoop, calls=%fused_computation | loop fusion | flops 327680 | bytes 491520 | tf_op jit(solution)/shard_map/scatter-add | solution.py:652
  124.4 0.6 slice.26
Async XLA Ops:
  83.5 22.4 %copy-start.2 = (s32[768]{0:T(1024)S(1)}, s32[768]{0:T(1024)}, u32[]{:S(2)}) copy-start(s32[768]{0:T(1024)} %starts.1) | copy-start | bytes 9220
  83.5 22.4 %copy-start.3 = (s32[768]{0:T(1024)S(1)}, s32[768]{0:T(1024)}, u32[]{:S(2)}) copy-start(s32[768]{0:T(1024)} %lengths.1) | copy-start | bytes 9220
  83.5 22.4 %copy-start.4 = (bf16[128,14]{0,1:T(8,128)(2,1)S(1)}, bf16[128,14]{0,1:T(8,128)(2,1)}, u32[]{:S(2)}) copy-start(bf16[128,14]{0,1:T(8,128)(2,1)} %param.20) | copy-start | bytes 10756
  105.9 1.3 %copy-start = (bf16[768,768]{1,0:T(8,128)(2,1)S(1)}, bf16[768,768]{1,0:T(8,128)(2,1)}, u32[]{:S(2)}) copy-start(bf16[768,768]{1,0:T(8,128)(2,1)} %shard_map.123.expanded) | copy-start | bytes 3538948
  107.2 3.8 %copy-start.1 = (s32[3968,14]{0,1:T(8,128)S(1)}, s32[3968,14]{0,1:T(8,128)}, u32[]{:S(2)}) copy-start(s32[3968,14]{0,1:T(8,128)} %param.23) | copy-start | bytes 666628

commit v3 on v2

--- a/solution.py
+++ b/solution.py
@@ -165,7 +165,7 @@
 def attend_kernel(
     tokens, gain, w_query, w_key, w_value, w_out, w_up, att, w_full, base,
     xb, weights, turned, up_in, up_turned, gains, qb, kb, vb, acc, top, o_send, l_send, o_recv, l_recv,
-    local, q_ss, q_rs, k_ss, k_rs, v_ss, v_rs, o_ss, o_rs, l_ss, l_rs, *sems,
+    local, q_ss, q_rs, k_ss, k_rs, v_ss, v_rs, far_ss, far_rs, o_ss, o_rs, l_ss, l_rs, *sems,
 ):
     x, y, z, core = coords()
     tok_ring = Gather(tokens, xb, TOK, CHUNKS, *sems[:6], wide=D // PARTS)
@@ -189,11 +189,22 @@
             src, dst, ss, rs = vb.at[h, 0, :, part], vb.at[h, slot, :, part], v_ss, v_rs
         return remote(src, dst, ss.at[h, slot, r], rs.at[h, slot, r], target)
 
-    def send(slots, r):
+    def send(r):
         for kind in "qkv":
-            for slot in slots:
+            for slot in (1, 2):
                 for h in range(2):
                     move(kind, h, slot, r).start()
+
+    def relay(kind, h, slot):
+        target = along(1 - h if kind == "q" else h, -offsets[slot])
+        part = pl.ds((slot - 1) * (TOK // 2), TOK // 2)
+        n = "qkv".index(kind)
+        buf = (qb, kb, vb)[n]
+        if kind == "k":
+            src, dst = buf.at[h, slot, part], buf.at[h, 3, part]
+        else:
+            src, dst = buf.at[h, slot, :, part], buf.at[h, 3, :, part]
+        return remote(src, dst, far_ss.at[n, h, slot - 1], far_rs.at[n, h, slot - 1], target)
 
     def lift(r):
         cut = pl.ds(r * STEP, STEP)
@@ -241,7 +252,7 @@
             qb[h, 0, :, cut] = (qkv[at : at + HD] * scale).astype(BF16)
             kb[h, 0, cut, :] = qkv[256 + at : 256 + at + HD].T.astype(BF16)
             vb[h, 0, :, cut] = qkv[512 + at : 512 + at + HD].astype(BF16)
-        send((1, 2), r)
+        send(r)
 
     turn(0)
     tok_ring.start(1, 2)
@@ -288,15 +299,29 @@
                     for r in range(CHUNKS):
                         move(kind, h, slot, r).wait_recv()
 
+        def arrivals(kinds, slot):
+            for kind in kinds:
+                for h in range(2):
+                    for r in range(CHUNKS):
+                        move(kind, h, slot, r).wait_recv()
+                    relay(kind, h, slot).start()
+
+        def far_arrivals(kinds):
+            for kind in kinds:
+                for h in range(2):
+                    for slot in (1, 2):
+                        relay(kind, h, slot).wait_recv()
+
+        for index, kinds, slot in ((1, "q", 1), (2, "q", 2), (3, "kv", 1), (4, "kv", 2)):
+            pl.when(i == index)(functools.partial(arrivals, kinds, slot))
+        for index, kinds in ((8, "q"), (11, "kv")):
+            pl.when(i == index)(functools.partial(far_arrivals, kinds))
+
         @pl.when(i == 1)
         def _():
-            for r in range(CHUNKS):
-                send((3,), r)
             lift(0)
             lift(1)
 
-        for index, kinds, slot in ((1, "q", 1), (2, "q", 2), (3, "kv", 1), (5, "kv", 2), (8, "q", 3), (11, "kv", 3)):
-            pl.when(i == index)(functools.partial(arrivals, kinds, slot))
         for r, index in enumerate((2, 5, 9, 12)):
             pl.when(i == index)(functools.partial(ring.forward, r))
         a = pick(i, [u[0] for u in UNITS])
@@ -350,10 +375,12 @@
     tok_ring.sent()
     ring.sent()
     for h in range(2):
-        for slot in range(1, 4):
+        for slot in (1, 2):
             for kind in "qkv":
                 for r in range(CHUNKS):
                     move(kind, h, slot, r).wait_send()
+                relay(kind, h, slot).wait_send()
+        for slot in range(1, 4):
             for copy in give(h, slot):
                 copy.wait_send()
 
@@ -387,6 +414,8 @@
             pltpu.VMEM((2, 3, 8, TOK), F32),
             dma((5 + KMER,)),
             *[dma((2, 4, CHUNKS)) for _ in range(6)],
+            dma((3, 2, 2)),
+            dma((3, 2, 2)),
             *[dma((2, 3)) for _ in range(4)],
             *gather_sems(CHUNKS),
             *gather_sems(PARTS_W),

time: 125 us -> 123 us (0.984)
  Pallas kernels: 121 us -> 118 us
    pallas_call x1, Pallas kernels: 82.9 us -> 78.4 us  [attend(): pl.pallas_call(attend_kernel, out_shape=(jax.ShapeDtypeStruct((TOK, 256),...]
    pallas_call x1, Pallas kernels: 11.8 us -> 13.9 us  [losses(): pl.pallas_call(loss_kernel, out_shape=(jax.ShapeDtypeStruct((LEAD, HD), B...]
where the time goes in v3:
time: 123 us
  Pallas kernels  118 us (96%)
  local copies, waits for them, and re-layouts  1.9 us (2%)
  other arithmetic  1.63 us (1%)
    pallas_call x1, Pallas kernels, attend(): pl.pallas_call(attend_kernel, out_shape=(jax.ShapeDtypeStruct((TOK, 256),...  78.4 us
    pallas_call x1, Pallas kernels, expand(): pl.pallas_call(expand_kernel, out_shape=jax.ShapeDtypeStruct((TOK, KMER *...  22.3 us
    pallas_call x1, Pallas kernels, losses(): pl.pallas_call(loss_kernel, out_shape=(jax.ShapeDtypeStruct((LEAD, HD), B...  13.9 us
    pallas_call x1, Pallas kernels, place(): pl.pallas_call(place_kernel, out_shape=(jax.ShapeDtypeStruct((NUC, HD), B...  3.77 us

profile of v3, /device:TPU:1, one launch (start us, length us, event | category | flops | bytes accessed | tf_op | source)
XLA Modules:
  0.0 122.5 jit_solution(438120393237885190)
XLA Ops:
  0.6 78.4 %shard_map.122 = (bf16[768,256]{1,0:T(8,128)(2,1)}, bf16[8,256,2560]{2,1,0:T(8,128)(2,1)}, f32[768,768]{1,0:T(8,128)}) custom-call(bf16[320,768]{1,0:T(8,128)(2,1)} %bitcast.8, f32[20,128]{1,0:T(8,128)} %bitcast.10, bf16[2560,256]{1,0:T(8,128)(2,1)} %w_query.1, bf16[2560,256]{1,0:T(8,128)(2,1)} %w_key.1, bf16[2560,256]{1,0:T(8,128)(2,1)} %w_value.1, ...), custom_call_target="tpu_custom_call" | custom-call | tf_op jit(solution)/shard_map/pallas_call | solution.py:390
  79.0 0.0 copy-start.2
  79.0 0.0 copy-start.3
  79.0 0.0 copy-start.4
  79.0 22.3 %shard_map.123.expanded = bf16[768,768]{1,0:T(8,128)(2,1)} custom-call(bf16[768,256]{1,0:T(8,128)(2,1)} %get-tuple-element.23.att, f32[768,768]{1,0:T(8,128)} %get-tuple-element.24.base, bf16[8,256,2560]{2,1,0:T(8,128)(2,1)} %get-tuple-element.25.w_full, bf16[6,2560,128]{2,1,0:T(8,128)(2,1)} %w_up.3), custom_call_target="tpu_custom_call" | custom-call | tf_op jit(solution)/shard_map/pallas_call | solution.py:482
  101.3 0.0 copy-done.2
  101.4 0.0 copy-done.3
  101.4 0.0 copy-done.4
  101.4 0.0 copy-start
  101.4 1.3 %copy-done = bf16[768,768]{1,0:T(8,128)(2,1)S(1)} copy-done((bf16[768,768]{1,0:T(8,128)(2,1)S(1)}, bf16[768,768]{1,0:T(8,128)(2,1)}, u32[]{:S(2)}) %copy-start) | copy-done | bytes 1179672
  102.6 0.0 copy-start.1
  102.6 3.8 %shard_map.124 = (bf16[3968,128]{1,0:T(8,128)(2,1)}, bf16[640,128]{1,0:T(8,128)(2,1)S(1)}, bf16[8,16,512]{2,1,0:T(8,128)(2,1)S(1)}, bf16[16,640]{1,0:T(8,128)(2,1)S(1)}) custom-call(s32[768]{0:T(1024)S(1)} %copy-done.2, s32[768]{0:T(1024)S(1)} %copy-done.3, bf16[768,768]{1,0:T(8,128)(2,1)S(1)} %copy-done, bf16[14,128]{1,0:T(8,128)(2,1)S(1)} %bitcast.7), custom_call_target="tpu_custom_call" | custom-call | tf_op jit(solution)/shard_map/pallas_call | solution.py:533
  106.4 0.0 copy-done.1
  106.4 13.9 %shard_map.125 = (bf16[640,128]{1,0:T(8,128)(2,1)S(1)}, f32[8,8,512]{2,1,0:T(8,128)S(1)}) custom-call(bf16[640,128]{1,0:T(8,128)(2,1)S(1)} %get-tuple-element.27.lead, bf16[8,16,512]{2,1,0:T(8,128)(2,1)S(1)} %get-tuple-element.28.pieces, bf16[16,640]{1,0:T(8,128)(2,1)S(1)} %get-tuple-element.29.lead_logits, s32[14,3968]{1,0:T(8,128)S(1)} %bitcast.6), custom_call_target="tpu_custom_call" | custom-call | tf_op jit(solution)/shard_map/pallas_call | solution.py:651
  120.3 1.6 %add_dynamic-update-slice_fusion = bf16[3968,128]{1,0:T(8,128)(2,1)} fusion(bf16[3968,128]{1,0:T(8,128)(2,1)} %get-tuple-element.26, bf16[640,128]{1,0:T(8,128)(2,1)S(1)} %get-tuple-element.30), kind=kLoop, calls=%fused_computation | loop fusion | flops 327680 | bytes 491520 | tf_op jit(solution)/shard_map/scatter-add | solution.py:681
  121.9 0.6 slice.26
Async XLA Ops:
  79.0 22.4 %copy-start.2 = (s32[768]{0:T(1024)S(1)}, s32[768]{0:T(1024)}, u32[]{:S(2)}) copy-start(s32[768]{0:T(1024)} %starts.1) | copy-start | bytes 9220
  79.0 22.3 %copy-start.3 = (s32[768]{0:T(1024)S(1)}, s32[768]{0:T(1024)}, u32[]{:S(2)}) copy-start(s32[768]{0:T(1024)} %lengths.1) | copy-start | bytes 9220
  79.0 22.3 %copy-start.4 = (bf16[128,14]{0,1:T(8,128)(2,1)S(1)}, bf16[128,14]{0,1:T(8,128)(2,1)}, u32[]{:S(2)}) copy-start(bf16[128,14]{0,1:T(8,128)(2,1)} %param.20) | copy-start | bytes 10756
  101.4 1.3 %copy-start = (bf16[768,768]{1,0:T(8,128)(2,1)S(1)}, bf16[768,768]{1,0:T(8,128)(2,1)}, u32[]{:S(2)}) copy-start(bf16[768,768]{1,0:T(8,128)(2,1)} %shard_map.123.expanded) | copy-start | bytes 3538948
  102.6 3.8 %copy-start.1 = (s32[3968,14]{0,1:T(8,128)S(1)}, s32[3968,14]{0,1:T(8,128)}, u32[]{:S(2)}) copy-start(s32[3968,14]{0,1:T(8,128)} %param.23) | copy-start | bytes 666628

commit v4 on v3

--- a/solution.py
+++ b/solution.py
@@ -65,18 +65,15 @@
     def partners(self):
         return [self.up, self.down, self.sibling]
 
-    def cut(self, r, part):
-        if part is None:
-            return pl.ds(r * self.step, self.step)
-        half = self.step // 2
-        return pl.ds(r * self.step + part * half, half)
+    def cut(self, r):
+        return pl.ds(r * self.step, self.step)
 
     def mine(self, r):
-        cut = self.cut(r, None)
+        cut = self.cut(r)
         return self.src.at[:, cut] if self.wide else self.src.at[cut]
 
-    def at(self, slot, r, part=None):
-        cut = self.cut(r, part)
+    def at(self, slot, r):
+        cut = self.cut(r)
         if self.wide:
             return self.buf.at[pl.ds(pl.multiple_of(slot * self.wide, 16), self.wide), cut]
         return self.buf.at[slot, cut]
@@ -93,21 +90,19 @@
         slot = self.at(self.slots[1 + way], r)
         return remote(slot, slot, y_send.at[way, r], y_recv.at[way, r], self.toward(way))
 
-    def onward(self, way, r):
+    def onward(self, r):
         f_send, f_recv = self.sems[2:4]
-        slot = self.at(self.slots[1 + way], r, way)
-        return remote(slot, slot, f_send.at[way, r], f_recv.at[way, r], self.toward(way))
-
-    def far_arrived(self, way, r):
+        slot = self.at(self.slots[1 + r % 2], r)
+        return remote(slot, slot, f_send.at[r], f_recv.at[r], self.toward(r % 2))
+
+    def far_arrived(self, r):
         f_send, f_recv = self.sems[2:4]
-        slot = self.at(self.slots[3], r, way)
-        return remote(slot, slot, f_send.at[way, r], f_recv.at[way, r], self.toward(way))
+        slot = self.at(self.slots[3], r)
+        return remote(slot, slot, f_send.at[r], f_recv.at[r], self.toward(r % 2))
 
     def across(self, which, r, arriving=False):
         c_send, c_recv = self.sems[4:]
-        part = which - 3 if which >= 3 else None
-        slots = self.twins if arriving else self.slots
-        slot = self.at(slots[min(which, 3)], r, part)
+        slot = self.at((self.twins if arriving else self.slots)[which], r)
         src = self.mine(r) if which == 0 and not arriving else slot
         return remote(src, slot, c_send.at[which, r], c_recv.at[which, r], self.sibling)
 
@@ -118,32 +113,32 @@
             self.across(0, r).start()
 
     def forward(self, r):
-        for way in range(2):
+        for way in (r % 2, 1 - r % 2):
             self.arrived(way, r).wait_recv()
-            self.onward(way, r).start()
+            if way == r % 2:
+                self.onward(r).start()
             self.across(1 + way, r).start()
 
     def forward_far(self, r):
-        for way in range(2):
-            self.far_arrived(way, r).wait_recv()
-            self.across(3 + way, r).start()
+        self.far_arrived(r).wait_recv()
+        self.across(3, r).start()
 
     def complete(self, r):
-        for which in range(5):
+        for which in range(4):
             self.across(which, r, arriving=True).wait_recv()
 
     def sent(self):
         for r in range(self.chunks):
             for way in range(2):
                 self.around(way, r).wait_send()
-                self.onward(way, r).wait_send()
-            for which in range(5):
+            self.onward(r).wait_send()
+            for which in range(4):
                 self.across(which, r).wait_send()
 
 
 def gather_sems(chunks):
     dma = pltpu.SemaphoreType.DMA
-    return [dma((2, chunks)), dma((2, chunks)), dma((2, chunks)), dma((2, chunks)), dma((5, chunks)), dma((5, chunks))]
+    return [dma((2, chunks)), dma((2, chunks)), dma((chunks,)), dma((chunks,)), dma((4, chunks)), dma((4, chunks))]
 
 
 def pick(index, options):
@@ -154,21 +149,22 @@
 
 
 CHUNKS = 3
+RING = 2 * CHUNKS
 STEP = TOK // CHUNKS
 PARTS_W = 4
 UNITS = [
-    (0, 0), (1, 0), (2, 0), (1, 1), (2, 1), (1, 2), (2, 2), (0, 1),
-    (3, 0), (3, 1), (3, 2), (3, 3), (1, 3), (2, 3), (0, 2), (0, 3),
+    (0, 0), (1, 0), (2, 0), (1, 1), (2, 1), (1, 2), (2, 2), (3, 0),
+    (3, 1), (3, 2), (3, 3), (1, 3), (2, 3), (0, 1), (0, 2), (0, 3),
 ]
 
 
 def attend_kernel(
     tokens, gain, w_query, w_key, w_value, w_out, w_up, att, w_full, base,
-    xb, weights, turned, up_in, up_turned, gains, qb, kb, vb, acc, top, o_send, l_send, o_recv, l_recv,
+    xb, weights, turned, up_in, gains, qb, kb, vb, acc, top, o_send, l_send, o_recv, l_recv,
     local, q_ss, q_rs, k_ss, k_rs, v_ss, v_rs, far_ss, far_rs, o_ss, o_rs, l_ss, l_rs, *sems,
 ):
     x, y, z, core = coords()
-    tok_ring = Gather(tokens, xb, TOK, CHUNKS, *sems[:6], wide=D // PARTS)
+    tok_ring = Gather(tokens, xb, TOK, RING, *sems[:6], wide=D // PARTS)
     ring = Gather(w_out, w_full, 256, PARTS_W, *sems[6:])
 
     def along(axis, by):
@@ -208,7 +204,7 @@
 
     def lift(r):
         cut = pl.ds(r * STEP, STEP)
-        base[cut, :] = jnp.dot(up_turned[...], xb[:, cut], preferred_element_type=F32).T
+        base[cut, :] = jnp.dot(xb[:, cut].T, up_in[...], preferred_element_type=F32)
 
     own = pltpu.make_async_copy(
         tokens, xb.at[pl.ds(pl.multiple_of(tok_ring.own * (D // PARTS), 16), D // PARTS)], local.at[0]
@@ -223,7 +219,7 @@
     for load in ups:
         load.start()
     greet([along(a, by) for a in range(2) for by in (1, -1, 2)] + ring.partners())
-    tok_ring.start(0, 1)
+    tok_ring.start(0, 3)
     for i in range(D // HD):
         gains[pl.ds(i * HD, HD), :] = jnp.broadcast_to(gain[pl.ds(i, 1), :], (HD, HD)).T
 
@@ -232,14 +228,11 @@
         for j in range(D // 256):
             turned[pl.ds(i * 256, 256), pl.ds(j * 256, 256)] = weights[i, pl.ds(j * 256, 256), :].T
 
-    def turn_up(i):
-        for j in range(D // 256):
-            up_turned[pl.ds(i * 256, 256), pl.ds(j * 256, 256)] = up_in[pl.ds(j * 256, 256), pl.ds(i * 256, 256)].T
-
     scale = math.log2(math.e) / math.sqrt(HD)
 
     def heads(r):
-        tok_ring.complete(r)
+        tok_ring.complete(2 * r)
+        tok_ring.complete(2 * r + 1)
         cut = pl.ds(r * STEP, STEP)
         wide = xb[:, cut].astype(F32)
         centred = wide - jnp.mean(wide, axis=0, keepdims=True)
@@ -254,28 +247,29 @@
             vb[h, 0, :, cut] = qkv[512 + at : 512 + at + HD].astype(BF16)
         send(r)
 
-    turn(0)
-    tok_ring.start(1, 2)
-    turn(1)
-    turn(2)
+    for i in range(3):
+        turn(i)
+    top[...] = jnp.full(top.shape, -1e30, F32)
+    acc[...] = jnp.zeros(acc.shape, F32)
     own.wait()
-    tok_ring.forward(0)
-    tok_ring.start(2, 3)
+    for r in range(3):
+        tok_ring.forward(r)
+        tok_ring.start(r + 3, r + 4)
+    tok_ring.forward_far(0)
+    tok_ring.forward(3)
+    tok_ring.forward_far(1)
+    heads(0)
+    tok_ring.forward(4)
+    tok_ring.forward_far(2)
+    tok_ring.forward(5)
+    tok_ring.forward_far(3)
+    ring.start()
+    heads(1)
     for load in ups:
         load.wait()
-    turn_up(0)
-    top[...] = jnp.full(top.shape, -1e30, F32)
-    acc[...] = jnp.zeros(acc.shape, F32)
-    tok_ring.forward(1)
-    tok_ring.forward_far(0)
-    turn_up(1)
-    heads(0)
-    tok_ring.forward(2)
-    tok_ring.forward_far(1)
-    ring.start()
-    heads(1)
-    tok_ring.forward_far(2)
-    turn_up(2)
+    lift(0)
+    tok_ring.forward_far(4)
+    tok_ring.forward_far(5)
     heads(2)
 
     ones = jnp.ones((16, TOK), BF16)
@@ -314,16 +308,21 @@
 
         for index, kinds, slot in ((1, "q", 1), (2, "q", 2), (3, "kv", 1), (4, "kv", 2)):
             pl.when(i == index)(functools.partial(arrivals, kinds, slot))
-        for index, kinds in ((8, "q"), (11, "kv")):
+        for index, kinds in ((7, "q"), (10, "kv")):
             pl.when(i == index)(functools.partial(far_arrivals, kinds))
 
         @pl.when(i == 1)
         def _():
-            lift(0)
             lift(1)
 
-        for r, index in enumerate((2, 5, 9, 12)):
-            pl.when(i == index)(functools.partial(ring.forward, r))
+        for step, index, pair in (
+            (ring.forward, 9, 0), (ring.forward, 10, 1), (ring.forward_far, 14, 0),
+        ):
+            @pl.when(i == index)
+            def _(step=step, pair=pair):
+                step(2 * pair)
+                step(2 * pair + 1)
+
         a = pick(i, [u[0] for u in UNITS])
         b = pick(i, [u[1] for u in UNITS])
         scores = [
@@ -340,7 +339,7 @@
             acc[h, a] = acc[h, a] * factor[:1] + added
             top[h, a] = now
 
-        @pl.when(jnp.logical_and(i >= 11, i < 14))
+        @pl.when(jnp.logical_and(i >= 10, i < 13))
         def _():
             for h in range(2):
                 value, level = partial(h, a)
@@ -353,7 +352,7 @@
 
     lax.fori_loop(0, len(UNITS), unit, 0)
     lift(CHUNKS - 1)
-    for r in range(PARTS_W):
+    for r in range(PARTS_W - 2, PARTS_W):
         ring.forward_far(r)
     for h in range(2):
         value, level = partial(h, 0)
@@ -401,7 +400,6 @@
             pltpu.VMEM((3, D, 256), BF16),
             pltpu.VMEM((768, D), BF16),
             pltpu.VMEM((D, KMER * HD), BF16),
-            pltpu.VMEM((KMER * HD, D), BF16),
             pltpu.VMEM((D, HD), F32),
             pltpu.VMEM((2, 4, HD, TOK), BF16),
             pltpu.VMEM((2, 4, TOK, HD), BF16),
@@ -417,7 +415,7 @@
             dma((3, 2, 2)),
             dma((3, 2, 2)),
             *[dma((2, 3)) for _ in range(4)],
-            *gather_sems(CHUNKS),
+            *gather_sems(RING),
             *gather_sems(PARTS_W),
         ],
         compiler_params=pltpu.CompilerParams(
@@ -431,7 +429,7 @@
 
 
 def expand_kernel(att, base, w_full, w_up, out, blocks, wo_v, wu_v, base_v, joint, local, *sems):
-    ring = Gather(att, blocks, TOK, CHUNKS, *sems)
+    ring = Gather(att, blocks, TOK, RING, *sems)
     ups = [pltpu.make_async_copy(w_up.at[j], wu_v.at[:, pl.ds(j * HD, HD)], local.at[2 + j]) for j in range(KMER)]
     outs = [pltpu.make_async_copy(w_full.at[j], wo_v.at[j], local.at[8 + j]) for j in range(PARTS)]
     lifted = pltpu.make_async_copy(base, base_v, local.at[1])
@@ -439,7 +437,7 @@
     for load in [*ups, *outs, own, lifted]:
         load.start()
     greet(ring.partners())
-    ring.start(0, 1)
+    ring.start(0, 3)
     for load in ups:
         load.wait()
 
@@ -448,31 +446,34 @@
         joint[pl.ds(i * 256, 256), :] = jnp.dot(wo_v[i], wu_v[...], preferred_element_type=F32).astype(BF16)
 
     def finish(r):
-        ring.complete(r)
+        ring.complete(2 * r)
+        ring.complete(2 * r + 1)
         cut = pl.ds(r * STEP, STEP)
         joined = jnp.concatenate([blocks[j, cut, :] for j in range(PARTS)], axis=1)
         raised = base_v[cut, :] + jnp.dot(joined, joint[...], preferred_element_type=F32)
         out[cut, :] = gelu(raised).astype(BF16)
 
-    merge(0)
-    merge(1)
-    ring.start(1, 2)
-    merge(2)
-    merge(3)
-    ring.forward(0)
+    for i in range(4):
+        merge(i)
+    for r in range(3):
+        ring.forward(r)
+        ring.start(r + 3, r + 4)
     merge(4)
-    ring.start(2, 3)
     merge(5)
+    ring.forward_far(0)
+    ring.forward(3)
+    ring.forward_far(1)
     merge(6)
-    ring.forward(1)
-    ring.forward_far(0)
+    ring.forward(4)
+    ring.forward_far(2)
     merge(7)
     own.wait()
     lifted.wait()
-    ring.forward(2)
-    ring.forward_far(1)
+    ring.forward(5)
+    ring.forward_far(3)
     finish(0)
-    ring.forward_far(2)
+    ring.forward_far(4)
+    ring.forward_far(5)
     finish(1)
     finish(2)
     ring.sent()
@@ -491,7 +492,7 @@
             pltpu.VMEM((TOK, KMER * HD), F32),
             pltpu.VMEM((PARTS * 256, KMER * HD), BF16),
             pltpu.SemaphoreType.DMA((16,)),
-            *gather_sems(CHUNKS),
+            *gather_sems(RING),
         ],
         compiler_params=pltpu.CompilerParams(
             collective_id=2, has_side_effects=True, vmem_limit_bytes=56 << 20
@@ -597,10 +598,10 @@
 
     early_copy(mp).start()
     late_copy(mp).start()
+    shift = remote(lead, arriving, lead_ss, lead_rs, {"seq": before, "mp": mp})
+    shift.start()
     for d in range(1, PARTS):
         piece(d).start()
-    shift = remote(lead, arriving, lead_ss, lead_rs, {"seq": before, "mp": mp})
-    shift.start()
     lab_head.wait()
     lab_tail.wait()
     for d in range(1, PARTS):

time: 123 us -> 127 us (1.033)
  Pallas kernels: 118 us -> 122 us
    pallas_call x1, Pallas kernels: 22.3 us -> 25.7 us  [expand(): pl.pallas_call(expand_kernel, out_shape=jax.ShapeDtypeStruct((TOK, KMER *...]
    pallas_call x1, Pallas kernels: 13.9 us -> 15.6 us  [losses(): pl.pallas_call(loss_kernel, out_shape=(jax.ShapeDtypeStruct((LEAD, HD), B...]
where the time goes in v4:
time: 127 us
  Pallas kernels  122 us (96%)
  local copies, waits for them, and re-layouts  1.9 us (1%)
  other arithmetic  1.63 us (1%)
    pallas_call x1, Pallas kernels, attend(): pl.pallas_call(attend_kernel, out_shape=(jax.ShapeDtypeStruct((TOK, 256),...  77.2 us
    pallas_call x1, Pallas kernels, expand(): pl.pallas_call(expand_kernel, out_shape=jax.ShapeDtypeStruct((TOK, KMER *...  25.7 us
    pallas_call x1, Pallas kernels, losses(): pl.pallas_call(loss_kernel, out_shape=(jax.ShapeDtypeStruct((LEAD, HD), B...  15.6 us
    pallas_call x1, Pallas kernels, place(): pl.pallas_call(place_kernel, out_shape=(jax.ShapeDtypeStruct((NUC, HD), B...  3.77 us

profile of v4, /device:TPU:1, one launch (start us, length us, event | category | flops | bytes accessed | tf_op | source)
XLA Modules:
  0.0 126.5 jit_solution(17795518293373735059)
XLA Ops:
  0.6 77.2 %shard_map.122 = (bf16[768,256]{1,0:T(8,128)(2,1)}, bf16[8,256,2560]{2,1,0:T(8,128)(2,1)}, f32[768,768]{1,0:T(8,128)}) custom-call(bf16[320,768]{1,0:T(8,128)(2,1)} %bitcast.8, f32[20,128]{1,0:T(8,128)} %bitcast.10, bf16[2560,256]{1,0:T(8,128)(2,1)} %w_query.1, bf16[2560,256]{1,0:T(8,128)(2,1)} %w_key.1, bf16[2560,256]{1,0:T(8,128)(2,1)} %w_value.1, ...), custom_call_target="tpu_custom_call" | custom-call | tf_op jit(solution)/shard_map/pallas_call | solution.py:389
  77.8 0.0 copy-start.2
  77.8 0.0 copy-start.3
  77.8 0.0 copy-start.4
  77.8 25.7 %shard_map.123.expanded = bf16[768,768]{1,0:T(8,128)(2,1)} custom-call(bf16[768,256]{1,0:T(8,128)(2,1)} %get-tuple-element.23.att, f32[768,768]{1,0:T(8,128)} %get-tuple-element.24.base, bf16[8,256,2560]{2,1,0:T(8,128)(2,1)} %get-tuple-element.25.w_full, bf16[6,2560,128]{2,1,0:T(8,128)(2,1)} %w_up.3), custom_call_target="tpu_custom_call" | custom-call | tf_op jit(solution)/shard_map/pallas_call | solution.py:483
  103.6 0.0 copy-done.2
  103.6 0.0 copy-done.3
  103.6 0.0 copy-done.4
  103.6 0.0 copy-start
  103.6 1.3 copy-done
  104.9 0.0 copy-start.1
  104.9 3.8 %shard_map.124 = (bf16[3968,128]{1,0:T(8,128)(2,1)}, bf16[640,128]{1,0:T(8,128)(2,1)S(1)}, bf16[8,16,512]{2,1,0:T(8,128)(2,1)S(1)}, bf16[16,640]{1,0:T(8,128)(2,1)S(1)}) custom-call(s32[768]{0:T(1024)S(1)} %copy-done.2, s32[768]{0:T(1024)S(1)} %copy-done.3, bf16[768,768]{1,0:T(8,128)(2,1)S(1)} %copy-done, bf16[14,128]{1,0:T(8,128)(2,1)S(1)} %bitcast.7), custom_call_target="tpu_custom_call" | custom-call | tf_op jit(solution)/shard_map/pallas_call | solution.py:534
  108.7 0.0 copy-done.1
  108.7 15.6 %shard_map.125 = (bf16[640,128]{1,0:T(8,128)(2,1)S(1)}, f32[8,8,512]{2,1,0:T(8,128)S(1)}) custom-call(bf16[640,128]{1,0:T(8,128)(2,1)S(1)} %get-tuple-element.27.lead, bf16[8,16,512]{2,1,0:T(8,128)(2,1)S(1)} %get-tuple-element.28.pieces, bf16[16,640]{1,0:T(8,128)(2,1)S(1)} %get-tuple-element.29.lead_logits, s32[14,3968]{1,0:T(8,128)S(1)} %bitcast.6), custom_call_target="tpu_custom_call" | custom-call | tf_op jit(solution)/shard_map/pallas_call | solution.py:652
  124.3 1.6 %add_dynamic-update-slice_fusion = bf16[3968,128]{1,0:T(8,128)(2,1)} fusion(bf16[3968,128]{1,0:T(8,128)(2,1)} %get-tuple-element.26, bf16[640,128]{1,0:T(8,128)(2,1)S(1)} %get-tuple-element.30), kind=kLoop, calls=%fused_computation | loop fusion | flops 327680 | bytes 491520 | tf_op jit(solution)/shard_map/scatter-add | solution.py:682
  125.9 0.6 slice.26
Async XLA Ops:
  77.8 25.8 %copy-start.2 = (s32[768]{0:T(1024)S(1)}, s32[768]{0:T(1024)}, u32[]{:S(2)}) copy-start(s32[768]{0:T(1024)} %starts.1) | copy-start | bytes 9220
  77.8 25.8 %copy-start.3 = (s32[768]{0:T(1024)S(1)}, s32[768]{0:T(1024)}, u32[]{:S(2)}) copy-start(s32[768]{0:T(1024)} %lengths.1) | copy-start | bytes 9220
  77.8 25.8 %copy-start.4 = (bf16[128,14]{0,1:T(8,128)(2,1)S(1)}, bf16[128,14]{0,1:T(8,128)(2,1)}, u32[]{:S(2)}) copy-start(bf16[128,14]{0,1:T(8,128)(2,1)} %param.20) | copy-start | bytes 10756
  103.6 1.3 %copy-start = (bf16[768,768]{1,0:T(8,128)(2,1)S(1)}, bf16[768,768]{1,0:T(8,128)(2,1)}, u32[]{:S(2)}) copy-start(bf16[768,768]{1,0:T(8,128)(2,1)} %shard_map.123.expanded) | copy-start | bytes 3538948
  104.9 3.8 %copy-start.1 = (s32[3968,14]{0,1:T(8,128)S(1)}, s32[3968,14]{0,1:T(8,128)}, u32[]{:S(2)}) copy-start(s32[3968,14]{0,1:T(8,128)} %param.23) | copy-start | bytes 666628

commit v5 on v3

--- a/solution.py
+++ b/solution.py
@@ -164,7 +164,7 @@
 
 def attend_kernel(
     tokens, gain, w_query, w_key, w_value, w_out, w_up, att, w_full, base,
-    xb, weights, turned, up_in, up_turned, gains, qb, kb, vb, acc, top, o_send, l_send, o_recv, l_recv,
+    xb, weights, turned, up_in, gains, qb, kb, vb, acc, top, o_send, l_send, o_recv, l_recv,
     local, q_ss, q_rs, k_ss, k_rs, v_ss, v_rs, far_ss, far_rs, o_ss, o_rs, l_ss, l_rs, *sems,
 ):
     x, y, z, core = coords()
@@ -208,7 +208,7 @@
 
     def lift(r):
         cut = pl.ds(r * STEP, STEP)
-        base[cut, :] = jnp.dot(up_turned[...], xb[:, cut], preferred_element_type=F32).T
+        base[cut, :] = jnp.dot(xb[:, cut].T, up_in[...], preferred_element_type=F32)
 
     own = pltpu.make_async_copy(
         tokens, xb.at[pl.ds(pl.multiple_of(tok_ring.own * (D // PARTS), 16), D // PARTS)], local.at[0]
@@ -232,10 +232,6 @@
         for j in range(D // 256):
             turned[pl.ds(i * 256, 256), pl.ds(j * 256, 256)] = weights[i, pl.ds(j * 256, 256), :].T
 
-    def turn_up(i):
-        for j in range(D // 256):
-            up_turned[pl.ds(i * 256, 256), pl.ds(j * 256, 256)] = up_in[pl.ds(j * 256, 256), pl.ds(i * 256, 256)].T
-
     scale = math.log2(math.e) / math.sqrt(HD)
 
     def heads(r):
@@ -261,21 +257,16 @@
     own.wait()
     tok_ring.forward(0)
     tok_ring.start(2, 3)
-    for load in ups:
-        load.wait()
-    turn_up(0)
     top[...] = jnp.full(top.shape, -1e30, F32)
     acc[...] = jnp.zeros(acc.shape, F32)
     tok_ring.forward(1)
     tok_ring.forward_far(0)
-    turn_up(1)
     heads(0)
     tok_ring.forward(2)
     tok_ring.forward_far(1)
     ring.start()
     heads(1)
     tok_ring.forward_far(2)
-    turn_up(2)
     heads(2)
 
     ones = jnp.ones((16, TOK), BF16)
@@ -319,6 +310,8 @@
 
         @pl.when(i == 1)
         def _():
+            for load in ups:
+                load.wait()
             lift(0)
             lift(1)
 
@@ -401,7 +394,6 @@
             pltpu.VMEM((3, D, 256), BF16),
             pltpu.VMEM((768, D), BF16),
             pltpu.VMEM((D, KMER * HD), BF16),
-            pltpu.VMEM((KMER * HD, D), BF16),
             pltpu.VMEM((D, HD), F32),
             pltpu.VMEM((2, 4, HD, TOK), BF16),
             pltpu.VMEM((2, 4, TOK, HD), BF16),
@@ -600,11 +592,11 @@
     for d in range(1, PARTS):
         piece(d).start()
     shift = remote(lead, arriving, lead_ss, lead_rs, {"seq": before, "mp": mp})
-    shift.start()
     lab_head.wait()
     lab_tail.wait()
     for d in range(1, PARTS):
         piece(d).wait_recv()
+    shift.start()
     summed = pieces[mp].astype(F32)
     for d in range(1, PARTS):
         summed = summed + received[d - 1].astype(F32)

time: 123 us -> 122 us (level)
  no operation moved by 1% of the time
where the time goes in v5:
time: 122 us
  Pallas kernels  118 us (97%)
  local copies, waits for them, and re-layouts  1.9 us (2%)
  other arithmetic  1.63 us (1%)
    pallas_call x1, Pallas kernels, attend(): pl.pallas_call(attend_kernel, out_shape=(jax.ShapeDtypeStruct((TOK, 256),...  78.1 us
    pallas_call x1, Pallas kernels, expand(): pl.pallas_call(expand_kernel, out_shape=jax.ShapeDtypeStruct((TOK, KMER *...  22.3 us
    pallas_call x1, Pallas kernels, losses(): pl.pallas_call(loss_kernel, out_shape=(jax.ShapeDtypeStruct((LEAD, HD), B...  13.8 us
    pallas_call x1, Pallas kernels, place(): pl.pallas_call(place_kernel, out_shape=(jax.ShapeDtypeStruct((NUC, HD), B...  3.77 us

profile of v5, /device:TPU:1, one launch (start us, length us, event | category | flops | bytes accessed | tf_op | source)
XLA Modules:
  0.0 122.3 jit_solution(11758462023432406773)
XLA Ops:
  0.6 78.1 %shard_map.122 = (bf16[768,256]{1,0:T(8,128)(2,1)}, bf16[8,256,2560]{2,1,0:T(8,128)(2,1)}, f32[768,768]{1,0:T(8,128)}) custom-call(bf16[320,768]{1,0:T(8,128)(2,1)} %bitcast.8, f32[20,128]{1,0:T(8,128)} %bitcast.10, bf16[2560,256]{1,0:T(8,128)(2,1)} %w_query.1, bf16[2560,256]{1,0:T(8,128)(2,1)} %w_key.1, bf16[2560,256]{1,0:T(8,128)(2,1)} %w_value.1, ...), custom_call_target="tpu_custom_call" | custom-call | tf_op jit(solution)/shard_map/pallas_call | solution.py:383
  78.8 0.0 copy-start.2
  78.8 0.0 copy-start.3
  78.8 0.0 copy-start.4
  78.8 22.3 %shard_map.123.expanded = bf16[768,768]{1,0:T(8,128)(2,1)} custom-call(bf16[768,256]{1,0:T(8,128)(2,1)} %get-tuple-element.23.att, f32[768,768]{1,0:T(8,128)} %get-tuple-element.24.base, bf16[8,256,2560]{2,1,0:T(8,128)(2,1)} %get-tuple-element.25.w_full, bf16[6,2560,128]{2,1,0:T(8,128)(2,1)} %w_up.3), custom_call_target="tpu_custom_call" | custom-call | tf_op jit(solution)/shard_map/pallas_call | solution.py:474
  101.1 0.0 copy-done.2
  101.1 0.0 copy-done.3
  101.1 0.0 copy-done.4
  101.1 0.0 copy-start
  101.1 1.3 %copy-done = bf16[768,768]{1,0:T(8,128)(2,1)S(1)} copy-done((bf16[768,768]{1,0:T(8,128)(2,1)S(1)}, bf16[768,768]{1,0:T(8,128)(2,1)}, u32[]{:S(2)}) %copy-start) | copy-done | bytes 1179672
  102.4 0.0 copy-start.1
  102.4 3.8 %shard_map.124 = (bf16[3968,128]{1,0:T(8,128)(2,1)}, bf16[640,128]{1,0:T(8,128)(2,1)S(1)}, bf16[8,16,512]{2,1,0:T(8,128)(2,1)S(1)}, bf16[16,640]{1,0:T(8,128)(2,1)S(1)}) custom-call(s32[768]{0:T(1024)S(1)} %copy-done.2, s32[768]{0:T(1024)S(1)} %copy-done.3, bf16[768,768]{1,0:T(8,128)(2,1)S(1)} %copy-done, bf16[14,128]{1,0:T(8,128)(2,1)S(1)} %bitcast.7), custom_call_target="tpu_custom_call" | custom-call | tf_op jit(solution)/shard_map/pallas_call | solution.py:525
  106.2 0.0 copy-done.1
  106.2 13.8 %shard_map.125 = (bf16[640,128]{1,0:T(8,128)(2,1)S(1)}, f32[8,8,512]{2,1,0:T(8,128)S(1)}) custom-call(bf16[640,128]{1,0:T(8,128)(2,1)S(1)} %get-tuple-element.27.lead, bf16[8,16,512]{2,1,0:T(8,128)(2,1)S(1)} %get-tuple-element.28.pieces, bf16[16,640]{1,0:T(8,128)(2,1)S(1)} %get-tuple-element.29.lead_logits, s32[14,3968]{1,0:T(8,128)S(1)} %bitcast.6), custom_call_target="tpu_custom_call" | custom-call | tf_op jit(solution)/shard_map/pallas_call | solution.py:643
  120.0 1.6 %add_dynamic-update-slice_fusion = bf16[3968,128]{1,0:T(8,128)(2,1)} fusion(bf16[3968,128]{1,0:T(8,128)(2,1)} %get-tuple-element.26, bf16[640,128]{1,0:T(8,128)(2,1)S(1)} %get-tuple-element.30), kind=kLoop, calls=%fused_computation | loop fusion | flops 327680 | bytes 491520 | tf_op jit(solution)/shard_map/scatter-add | solution.py:673
  121.6 0.6 slice.26
Async XLA Ops:
  78.8 22.4 %copy-start.2 = (s32[768]{0:T(1024)S(1)}, s32[768]{0:T(1024)}, u32[]{:S(2)}) copy-start(s32[768]{0:T(1024)} %starts.1) | copy-start | bytes 9220
  78.8 22.3 %copy-start.3 = (s32[768]{0:T(1024)S(1)}, s32[768]{0:T(1024)}, u32[]{:S(2)}) copy-start(s32[768]{0:T(1024)} %lengths.1) | copy-start | bytes 9220
  78.8 22.3 %copy-start.4 = (bf16[128,14]{0,1:T(8,128)(2,1)S(1)}, bf16[128,14]{0,1:T(8,128)(2,1)}, u32[]{:S(2)}) copy-start(bf16[128,14]{0,1:T(8,128)(2,1)} %param.20) | copy-start | bytes 10756
  101.1 1.3 %copy-start = (bf16[768,768]{1,0:T(8,128)(2,1)S(1)}, bf16[768,768]{1,0:T(8,128)(2,1)}, u32[]{:S(2)}) copy-start(bf16[768,768]{1,0:T(8,128)(2,1)} %shard_map.123.expanded) | copy-start | bytes 3538948
  102.4 3.8 %copy-start.1 = (s32[3968,14]{0,1:T(8,128)S(1)}, s32[3968,14]{0,1:T(8,128)}, u32[]{:S(2)}) copy-start(s32[3968,14]{0,1:T(8,128)} %param.23) | copy-start | bytes 666628

commit v6 on v5

--- a/solution.py
+++ b/solution.py
@@ -491,14 +491,20 @@
     )(att, base, w_full, w_up)
 
 
-def place_kernel(starts, lengths, expanded, w_class, own, lead, logits, lead_logits, wide, placed, classes):
-    for j in range(KMER):
-        wide[pl.ds(j, TOK, stride=8), :] = expanded[:, j * HD : (j + 1) * HD].astype(F32)
+def place_kernel(starts, lengths, expanded, w_class, own, lead, logits, lead_logits, wide, placed, classes, part, sems):
+    loads = [
+        pltpu.make_async_copy(expanded.at[:, pl.ds(j * HD, HD)], part.at[j], sems.at[j]) for j in range(KMER)
+    ]
+    for load in loads:
+        load.start()
     placed[:LEAD, :] = jnp.zeros((LEAD, HD), F32)
     placed[NUC:, :] = jnp.zeros((LEAD + 16, HD), F32)
     classes[...] = jnp.zeros(classes.shape, F32)
     classes[:CLASSES, :] = w_class[...].astype(F32)
     shift = LEAD - lax.axis_index("seq") * NUC
+    for j in range(KMER):
+        loads[j].wait()
+        wide[pl.ds(j, TOK, stride=8), :] = part[j].astype(F32)
 
     def one(t, carry):
         placed[pl.ds(starts[t] + shift, 8), :] = wide[pl.ds(pl.multiple_of(t * 8, 8), 8), :]
@@ -530,12 +536,14 @@
             jax.ShapeDtypeStruct((PARTS, 16, PIECE), BF16),
             jax.ShapeDtypeStruct((16, LEAD), BF16),
         ),
-        in_specs=[SMEM, SMEM, VMEM, VMEM],
+        in_specs=[SMEM, SMEM, ANY, VMEM],
         out_specs=(VMEM, VMEM, VMEM, VMEM),
         scratch_shapes=[
             pltpu.VMEM((TOK * 8, HD), F32),
             pltpu.VMEM((LEAD + NUC + 16, HD), F32),
             pltpu.VMEM((16, HD), F32),
+            pltpu.VMEM((KMER, TOK, HD), BF16),
+            pltpu.SemaphoreType.DMA((KMER,)),
         ],
         compiler_params=pltpu.CompilerParams(vmem_limit_bytes=48 << 20),
     )(starts, lengths, expanded, w_class)
@@ -591,12 +599,18 @@
     late_copy(mp).start()
     for d in range(1, PARTS):
         piece(d).start()
-    shift = remote(lead, arriving, lead_ss, lead_rs, {"seq": before, "mp": mp})
+    shifts = []
+    for i in range(2):
+        part = pl.ds(i * (LEAD // 2), LEAD // 2)
+        shifts.append(
+            remote(lead.at[part], arriving.at[part], lead_ss.at[i], lead_rs.at[i], {"seq": before, "mp": mp})
+        )
+    shifts[0].start()
     lab_head.wait()
     lab_tail.wait()
     for d in range(1, PARTS):
         piece(d).wait_recv()
-    shift.start()
+    shifts[1].start()
     summed = pieces[mp].astype(F32)
     for d in range(1, PARTS):
         summed = summed + received[d - 1].astype(F32)
@@ -629,7 +643,8 @@
     loss[mp] = mine[...]
     for d in range(1, PARTS):
         spread(d).wait_recv()
-    shift.wait()
+    for shift in shifts:
+        shift.wait()
     early_copy(mp).wait_send()
     late_copy(mp).wait_send()
     for d in range(1, PARTS):
@@ -655,7 +670,7 @@
             pltpu.VMEM((16, PIECE), F32),
             pltpu.VMEM((CLASSES, PIECE), jnp.int32),
             pltpu.VMEM((8, PIECE), F32),
-            dma, dma, dma((7,)), dma((7,)), dma, dma((PARTS,)), dma, dma((PARTS,)), dma((7,)), dma((7,)), dma((2,)),
+            dma((2,)), dma((2,)), dma((7,)), dma((7,)), dma, dma((PARTS,)), dma, dma((PARTS,)), dma((7,)), dma((7,)), dma((2,)),
         ],
         compiler_params=pltpu.CompilerParams(
             collective_id=3, has_side_effects=True, vmem_limit_bytes=32 << 20

time: 122 us -> 123 us (level)
  no operation moved by 1% of the time
where the time goes in v6:
time: 123 us
  Pallas kernels  118 us (96%)
  local copies, waits for them, and re-layouts  1.9 us (2%)
  other arithmetic  1.63 us (1%)
    pallas_call x1, Pallas kernels, attend(): pl.pallas_call(attend_kernel, out_shape=(jax.ShapeDtypeStruct((TOK, 256),...  78.1 us
    pallas_call x1, Pallas kernels, expand(): pl.pallas_call(expand_kernel, out_shape=jax.ShapeDtypeStruct((TOK, KMER *...  22.3 us
    pallas_call x1, Pallas kernels, losses(): pl.pallas_call(loss_kernel, out_shape=(jax.ShapeDtypeStruct((LEAD, HD), B...  14 us
    pallas_call x1, Pallas kernels, place(): pl.pallas_call(place_kernel, out_shape=(jax.ShapeDtypeStruct((NUC, HD), B...  4.08 us

profile of v6, /device:TPU:1, one launch (start us, length us, event | category | flops | bytes accessed | tf_op | source)
XLA Modules:
  0.0 122.7 jit_solution(15994249674906766069)
XLA Ops:
  0.6 78.1 %shard_map.122 = (bf16[768,256]{1,0:T(8,128)(2,1)}, bf16[8,256,2560]{2,1,0:T(8,128)(2,1)}, f32[768,768]{1,0:T(8,128)}) custom-call(bf16[320,768]{1,0:T(8,128)(2,1)} %bitcast.8, f32[20,128]{1,0:T(8,128)} %bitcast.10, bf16[2560,256]{1,0:T(8,128)(2,1)} %w_query.1, bf16[2560,256]{1,0:T(8,128)(2,1)} %w_key.1, bf16[2560,256]{1,0:T(8,128)(2,1)} %w_value.1, ...), custom_call_target="tpu_custom_call" | custom-call | tf_op jit(solution)/shard_map/pallas_call | solution.py:383
  78.8 0.0 copy-start.2
  78.8 0.0 copy-start.3
  78.8 0.0 copy-start.4
  78.8 22.3 %shard_map.123.expanded = bf16[768,768]{1,0:T(8,128)(2,1)} custom-call(bf16[768,256]{1,0:T(8,128)(2,1)} %get-tuple-element.23.att, f32[768,768]{1,0:T(8,128)} %get-tuple-element.24.base, bf16[8,256,2560]{2,1,0:T(8,128)(2,1)} %get-tuple-element.25.w_full, bf16[6,2560,128]{2,1,0:T(8,128)(2,1)} %w_up.3), custom_call_target="tpu_custom_call" | custom-call | tf_op jit(solution)/shard_map/pallas_call | solution.py:474
  101.1 0.0 copy-done.2
  101.1 0.0 copy-done.3
  101.1 0.0 copy-done.4
  101.1 0.0 copy-start
  101.1 1.3 %copy-done = bf16[768,768]{1,0:T(8,128)(2,1)S(1)} copy-done((bf16[768,768]{1,0:T(8,128)(2,1)S(1)}, bf16[768,768]{1,0:T(8,128)(2,1)}, u32[]{:S(2)}) %copy-start) | copy-done | bytes 1179672
  102.4 0.0 copy-start.1
  102.4 4.1 %shard_map.124 = (bf16[3968,128]{1,0:T(8,128)(2,1)}, bf16[640,128]{1,0:T(8,128)(2,1)S(1)}, bf16[8,16,512]{2,1,0:T(8,128)(2,1)S(1)}, bf16[16,640]{1,0:T(8,128)(2,1)S(1)}) custom-call(s32[768]{0:T(1024)S(1)} %copy-done.2, s32[768]{0:T(1024)S(1)} %copy-done.3, bf16[768,768]{1,0:T(8,128)(2,1)S(1)} %copy-done, bf16[14,128]{1,0:T(8,128)(2,1)S(1)} %bitcast.7), custom_call_target="tpu_custom_call" | custom-call | tf_op jit(solution)/shard_map/pallas_call | solution.py:531
  106.5 0.0 copy-done.1
  106.5 14.0 %shard_map.125 = (bf16[640,128]{1,0:T(8,128)(2,1)S(1)}, f32[8,8,512]{2,1,0:T(8,128)S(1)}) custom-call(bf16[640,128]{1,0:T(8,128)(2,1)S(1)} %get-tuple-element.27.lead, bf16[8,16,512]{2,1,0:T(8,128)(2,1)S(1)} %get-tuple-element.28.pieces, bf16[16,640]{1,0:T(8,128)(2,1)S(1)} %get-tuple-element.29.lead_logits, s32[14,3968]{1,0:T(8,128)S(1)} %bitcast.6), custom_call_target="tpu_custom_call" | custom-call | tf_op jit(solution)/shard_map/pallas_call | solution.py:658
  120.5 1.6 %add_dynamic-update-slice_fusion = bf16[3968,128]{1,0:T(8,128)(2,1)} fusion(bf16[3968,128]{1,0:T(8,128)(2,1)} %get-tuple-element.26, bf16[640,128]{1,0:T(8,128)(2,1)S(1)} %get-tuple-element.30), kind=kLoop, calls=%fused_computation | loop fusion | flops 327680 | bytes 491520 | tf_op jit(solution)/shard_map/scatter-add | solution.py:688
  122.1 0.6 slice.26
Async XLA Ops:
  78.8 22.4 %copy-start.2 = (s32[768]{0:T(1024)S(1)}, s32[768]{0:T(1024)}, u32[]{:S(2)}) copy-start(s32[768]{0:T(1024)} %starts.1) | copy-start | bytes 9220
  78.8 22.3 %copy-start.3 = (s32[768]{0:T(1024)S(1)}, s32[768]{0:T(1024)}, u32[]{:S(2)}) copy-start(s32[768]{0:T(1024)} %lengths.1) | copy-start | bytes 9220
  78.8 22.3 %copy-start.4 = (bf16[128,14]{0,1:T(8,128)(2,1)S(1)}, bf16[128,14]{0,1:T(8,128)(2,1)}, u32[]{:S(2)}) copy-start(bf16[128,14]{0,1:T(8,128)(2,1)} %param.20) | copy-start | bytes 10756
  101.1 1.3 %copy-start = (bf16[768,768]{1,0:T(8,128)(2,1)S(1)}, bf16[768,768]{1,0:T(8,128)(2,1)}, u32[]{:S(2)}) copy-start(bf16[768,768]{1,0:T(8,128)(2,1)} %shard_map.123.expanded) | copy-start | bytes 3538948
  102.4 4.1 %copy-start.1 = (s32[3968,14]{0,1:T(8,128)S(1)}, s32[3968,14]{0,1:T(8,128)}, u32[]{:S(2)}) copy-start(s32[3968,14]{0,1:T(8,128)} %param.23) | copy-start | bytes 666628
